TPU v7x, 128 devices: a whole 4x4x4 slice. The times are simulated.
128 devices in a mesh: seq: 32 (over x, y, core), head: 4 (over z).
Axes of the slice: x: 4, y: 4, z: 4, core: 2. Of those that a mesh axis runs over, the one named last changes fastest.
Arguments:
- queries: bfloat16 [98304, 4096], P('seq', 'head'), may hold values from -6 to 6
- keys: bfloat16 [98304, 4096], P('seq', 'head'), may hold values from -6 to 6
- values: bfloat16 [98304, 4096], P('seq', 'head'), may hold values from -40 to 40
- gain: float32 [4096], P('head'), may hold values from 0.1 to 1.9
- placement: int32 [768], P('seq'), may hold values from 0 to 767, as said below
- segments: int32 [768], P('seq'), may hold values from 0 to 7, never falling along the last dimension, each value on 1 to 192 neighbouring positions
Outputs:
- scored: bfloat16 [98304, 4096], P('seq', 'head')
Inputs may be any that keep to these rules, and one draw needn't show every extreme that they name: `placement`: together a permutation of the 768 sequence blocks; the blocks of loader d are entries d * 24 to (d + 1) * 24 - 1, those of owner o are o * 24 to (o + 1) * 24 - 1; a loader holds exactly 1 block of every owner it holds any of, and none of the others. `segments`: never falling along the sequence; every document has 1 to 192 blocks.
All inputs are finite; a program needn't handle non-finite values.
Results may differ from a plain program's by a relative error of at most 0.0049.
Values may be sent and summed in bfloat16 or wider, within the bound.
No kernel may reach another device: no remote copies, remote signals or barrier semaphores. Data moves between devices by JAX's collectives and lax.ppermute only.
A program may use at most 192 MiB of HBM per device.

v0:
```python
import jax
import jax.numpy as jnp
from jax import lax
from jax.sharding import PartitionSpec as P

HD = 128
BLOCK = 128
BLOCKS_DEV = 24


def prefix(value, axis, join, neutral):
    count, mine = (lax.axis_size(axis), lax.axis_index(axis))
    pieces = jax.tree.map(lambda part: lax.all_gather(part, axis), value)
    subtotal = jax.tree.map(
        lambda part, zero: jnp.full_like(part, 0) + jnp.asarray(zero, part.dtype), value, neutral
    )

    def step(position, subtotal):
        longer = join(subtotal, jax.tree.map(lambda part: part[position], pieces))
        return jax.tree.map(lambda new, old: jnp.where(position < mine, new, old), longer, subtotal)

    return lax.fori_loop(0, count - 1, step, subtotal)


def slot_plan(placement):
    seq_count = lax.axis_size("seq")
    slot_cap = (BLOCKS_DEV + seq_count - 1) // seq_count
    owner_of = placement // BLOCKS_DEV
    within_owner = placement % BLOCKS_DEV
    positions = jnp.arange(BLOCKS_DEV, dtype=jnp.int32)
    earlier = (positions[None, :] < positions[:, None]) & (owner_of[None, :] == owner_of[:, None])
    rank_index = jnp.sum(earlier.astype(jnp.int32), axis=1)
    slot_index = owner_of * slot_cap + rank_index
    all_slots = jnp.arange(seq_count * slot_cap, dtype=jnp.int32)
    matches = slot_index[None, :] == all_slots[:, None]
    source_index = jnp.sum(matches.astype(jnp.int32) * positions[None, :], axis=1)
    filled = jnp.any(matches, axis=1)
    owner_label = jnp.where(filled, jnp.take(within_owner, source_index), -1)
    return (slot_index, source_index, filled, owner_label)


def owner_pick(labels):
    positions = jnp.arange(BLOCKS_DEV, dtype=jnp.int32)
    all_slots = jnp.arange(labels.shape[0], dtype=jnp.int32)
    matches = labels[None, :] == positions[:, None]
    return jnp.sum(matches.astype(jnp.int32) * all_slots[None, :], axis=1)


def pack_slots(data, source_index, filled):
    picked = jnp.take(data, source_index, axis=0)
    keep_mask = filled.reshape((-1,) + (1,) * (data.ndim - 1))
    return jnp.where(keep_mask, picked, jnp.zeros((), data.dtype))


def return_slots(own_rows, labels):
    picked = jnp.take(own_rows, jnp.maximum(labels, 0), axis=0)
    keep_mask = (labels >= 0).reshape((-1,) + (1,) * (own_rows.ndim - 1))
    return jnp.where(keep_mask, picked, jnp.zeros((), own_rows.dtype))


def combine_tails(early, later):
    early_state, early_seg = early
    later_state, later_seg = later
    joined = later_state + jnp.where(
        later_seg == early_seg, early_state, jnp.zeros_like(early_state)
    )
    return (
        jnp.where(later_seg < 0, early_state, joined),
        jnp.where(later_seg < 0, early_seg, later_seg),
    )


def carry_into(tail_state, last_seg):
    identity = (jnp.zeros_like(tail_state), jnp.full((), -1, jnp.int32))
    return prefix((tail_state, last_seg), "seq", combine_tails, identity)


def prefix_states(states, segments):
    positions = jnp.arange(states.shape[0], dtype=jnp.int32)
    before = (positions[None, :] < positions[:, None]) & (segments[None, :] == segments[:, None])
    inner_sum = jnp.einsum(
        "nm,mhde->nhde", before.astype(jnp.float32), states, precision=lax.Precision.HIGHEST
    )
    last_seg = segments[-1]
    tail_weights = (segments == last_seg).astype(jnp.float32)
    tail_state = jnp.einsum("m,mhde->hde", tail_weights, states, precision=lax.Precision.HIGHEST)
    incoming, prev_seg = carry_into(tail_state, last_seg)
    same_doc = (segments == prev_seg)[:, None, None, None]
    carried = inner_sum + jnp.where(same_doc, incoming[None], jnp.zeros((), jnp.float32))
    return carried.astype(jnp.bfloat16)


def block_states(key_rows, value_rows):
    return jnp.einsum("nshd,nshe->nhde", key_rows, value_rows, preferred_element_type=jnp.float32)


def local_part(query_rows, key_rows, value_rows):
    scores = jnp.einsum("nthd,nshd->nhts", query_rows, key_rows, preferred_element_type=jnp.float32)
    causal = jnp.tril(jnp.ones((BLOCK, BLOCK), dtype=bool))
    scores = jnp.where(causal[None, None], scores, jnp.zeros((), jnp.float32)).astype(jnp.bfloat16)
    return jnp.einsum("nhts,nshd->nthd", scores, value_rows, preferred_element_type=jnp.float32)


def cross_part(query_rows, carried):
    return jnp.einsum("nthd,nhde->nthe", query_rows, carried, preferred_element_type=jnp.float32)


def finish_rows(attended, gain):
    flat_rows = attended.reshape(
        attended.shape[0] * attended.shape[1], attended.shape[2] * attended.shape[3]
    )
    square_sum = lax.psum(jnp.sum(flat_rows * flat_rows, axis=1), "head")
    full_width = flat_rows.shape[1] * lax.axis_size("head")
    scaling = lax.rsqrt(square_sum / full_width + 1e-05)
    return (flat_rows * scaling[:, None] * gain[None, :]).astype(jnp.bfloat16)


def on_device(queries, keys, values, gain, placement, segments):
    block_count = queries.shape[0] // BLOCK
    features = queries.shape[1]
    head_count = features // HD
    slot_index, source_index, filled, owner_label = slot_plan(placement)
    query_blocks = pack_slots(queries.reshape(block_count, BLOCK, features), source_index, filled)
    key_blocks = pack_slots(keys.reshape(block_count, BLOCK, features), source_index, filled)
    value_blocks = pack_slots(values.reshape(block_count, BLOCK, features), source_index, filled)
    got_queries, got_keys, got_values, got_labels = (
        lax.all_to_all(query_blocks, "seq", split_axis=0, concat_axis=0, tiled=True),
        lax.all_to_all(key_blocks, "seq", split_axis=0, concat_axis=0, tiled=True),
        lax.all_to_all(value_blocks, "seq", split_axis=0, concat_axis=0, tiled=True),
        lax.all_to_all(owner_label, "seq", split_axis=0, concat_axis=0, tiled=True),
    )
    pick_slot = owner_pick(got_labels)
    query_rows = jnp.take(got_queries, pick_slot, axis=0).reshape(
        block_count, BLOCK, head_count, HD
    )
    key_rows = jnp.take(got_keys, pick_slot, axis=0).reshape(block_count, BLOCK, head_count, HD)
    value_rows = jnp.take(got_values, pick_slot, axis=0).reshape(block_count, BLOCK, head_count, HD)
    carried = prefix_states(block_states(key_rows, value_rows), segments)
    attended = local_part(query_rows, key_rows, value_rows) + cross_part(query_rows, carried)
    scored_rows = finish_rows(attended, gain).reshape(block_count, BLOCK, features)
    returned = lax.all_to_all(
        return_slots(scored_rows, got_labels), "seq", split_axis=0, concat_axis=0, tiled=True
    )
    return jnp.take(returned, slot_index, axis=0).reshape(block_count * BLOCK, features)


def solution(mesh):
    return jax.shard_map(
        on_device,
        mesh=mesh,
        in_specs=(
            P("seq", "head"),
            P("seq", "head"),
            P("seq", "head"),
            P("head"),
            P("seq"),
            P("seq"),
        ),
        out_specs=P("seq", "head"),
        check_vma=False,
    )
```

profile of v0, /device:TPU:8, one launch (start us, length us, event | category | flops | bytes accessed | tf_op | source)
XLA Modules:
  0.0 887.8 jit_solution(4408909231920217157)
XLA Ops:
  24.4 7.8 gather_fusion.5
  39.9 16.5 %select_select_fusion.4 = (bf16[32,128,1024]{2,1,0:T(8,128)(2,1)}, bf16[32,128,1024]{2,1,0:T(8,128)(2,1)}, bf16[32,128,1024]{2,1,0:T(8,128)(2,1)}) fusion(bf16[32,128,1024]{2,1,0:T(8,128)(2,1)} %gather_fusion.1, pred[32]{0:T(512)(128)(4,1)S(1)} %compare_and_fusion.2, pred[32]{0:T(512)(128)(4,1)S(1)} %fusion.17, bf16[32,128,1024]{2,1,0:T(8,128)(2,1)} %gather_fusion.3, ...), kind=kLoop, calls=%fused_computation.24 | loop fusion | flops 25165824 | bytes 50331712 | tf_op jit(solution)/shard_map/jit(_where)/select_n | solution.py:52
  56.5 102.0 %all_to_all.26 = bf16[32,128,1024]{2,1,0:T(8,128)(2,1)} all-to-all(bf16[32,128,1024]{2,1,0:T(8,128)(2,1)} %get-tuple-element.155), channel_id=1, replica_groups=mesh['seq'=32,'head'=4] {'seq'}, dimensions={0} | all-to-all | bytes 16777216 | tf_op jit(solution)/shard_map/all_to_all | solution.py:127
  158.4 99.4 %all_to_all.27 = bf16[32,128,1024]{2,1,0:T(8,128)(2,1)} all-to-all(bf16[32,128,1024]{2,1,0:T(8,128)(2,1)S(1)} %copy-done), channel_id=1, replica_groups=mesh['seq'=32,'head'=4] {'seq'}, dimensions={0} | all-to-all | bytes 16777216 | tf_op jit(solution)/shard_map/all_to_all | solution.py:128
  274.6 7.8 gather_fusion.6
  282.4 105.7 %all-to-all-done.1 = bf16[32,128,1024]{2,1,0:T(8,128)(2,1)} async-done(((bf16[32,128,1024]{2,1,0:T(8,128)(2,1)}), bf16[32,128,1024]{2,1,0:T(8,128)(2,1)}, u32[]{:S(2)}, u32[]{:S(2)}) %all-to-all-start.1) | async-done | bytes 8388640 | tf_op jit(solution)/shard_map/all_to_all | solution.py:129
  388.0 7.9 gather_fusion.2
  395.9 14.0 %broadcast_select_fusion.3 = (bf16[24,128,1024]{2,1,0:T(8,128)(2,1)}, bf16[24,128,1024]{2,1,0:T(8,128)(2,1)}, bf16[24,128,1024]{2,1,0:T(8,128)(2,1)}) fusion(bf16[24,128,1024]{2,1,0:T(8,128)(2,1)} %gather_fusion.2, pred[24]{0:T(512)(128)(4,1)S(1)} %compare_and_fusion.1, bf16[24,128,1024]{2,1,0:T(8,128)(2,1)} %gather_fusion.4, ...), kind=kLoop, calls=%fused_computation.33 | loop fusion | flops 9437184 | bytes 37748760 | tf_op jit(solution)/shard_map/jit(_take)/select_n | solution.py:137
  409.9 8.7 copy.75
  418.6 8.6 copy.57
  427.2 13.6 %fusion.32 = f32[24,8,128,128]{3,2,1,0:T(8,128)} fusion(bf16[24,128,8,128]{1,3,2,0:T(8,128)(2,1)} %bitcast.58, bf16[24,128,8,128]{1,3,2,0:T(8,128)(2,1)} %bitcast.60), kind=kOutput, calls=%fused_computation.82 | convolution fusion | flops 805306368 | bytes 25165824 | tf_op jit(solution)/shard_map/nshd,nshe->nhde/dot_general | solution.py:94
  440.8 17.2 %fusion.2 = f32[1,8,128,128]{3,0,2,1:T(1,128)} fusion(f32[24,8,128,128]{3,2,1,0:T(8,128)} %fusion.32, s32[24]{0:T(128)S(1)} %copy-done.1, s32[]{:T(128)} %bitcast.14), kind=kOutput, calls=%fused_computation.17 | convolution fusion | flops 37748760 | bytes 13107300 | tf_op jit(solution)/shard_map/m,mhde->hde/dot_general | solution.py:86
  458.0 10.8 %all-reduce = s32[32]{0:T(128)S(1)} all-reduce(s32[32]{0:T(128)S(1)} %get-tuple-element.158), channel_id=1, replica_groups=mesh['seq'=32,'head'=4] {'seq'}, use_global_device_ids=true, to_apply=%add | all-reduce | flops 32 | bytes 256
  469.0 8.8 copy.58
  477.8 19.7 %fusion.4 = f32[24,8,128,128]{3,0,2,1:T(8,128)} fusion(f32[24,8,128,128]{3,2,1,0:T(8,128)} %fusion.32, s32[24]{0:T(128)S(1)} %copy-done.1), kind=kOutput, calls=%fused_computation.19 | convolution fusion | flops 905971392 | bytes 25165920 | tf_op jit(solution)/shard_map/nm,mhde->nhde/dot_general | solution.py:81
  497.5 33.6 %all-gather.3.cloned.1.call-done = f32[256,128,128]{2,1,0:T(8,128)} async-done(((f32[8,128,128]{2,1,0:T(8,128)}), f32[256,128,128]{2,1,0:T(8,128)}) %all-gather.3.cloned.1.call-update) | async-done | bytes 16777232 | tf_op jit(solution)/shard_map/all_gather | solution.py:13
  531.1 118.0 %while.16 = (s32[]{:T(128)}, f32[8,128,128]{2,1,0:T(8,128)S(1)}, s32[]{:T(128)}, s32[]{:T(128)}, s32[32]{0:T(128)S(1)}, /*index=5*/f32[32,8,128,128]{3,2,1,0:T(8,128)}, s32[]{:T(128)}, s32[]{:T(128)}) while((s32[]{:T(128)}, f32[8,128,128]{2,1,0:T(8,128)S(1)}, s32[]{:T(128)}, s32[]{:T(128)}, s32[32]{0:T(128)S(1)}, ...), condition=%wide.region_5.8_spmd.clone, body=%wide.region_4.7_spmd.clone.sunk | while | flops 655368 | bytes 1573031 | solution.py:22
  649.1 16.0 %fusion.7 = f32[24,8,128,128]{3,2,1,0:T(8,128)} fusion(bf16[24,128,8,128]{1,3,2,0:T(8,128)(2,1)} %bitcast.62, f32[24,8,128,128]{3,0,2,1:T(8,128)} %fusion.4, f32[8,128,128]{2,1,0:T(8,128)S(1)} %get-tuple-element.118, pred[24]{0:T(512)(128)(4,1)S(1)} %broadcast_compare_fusion.1), kind=kOutput, calls=%fused_computation.26 | convolution fusion | flops 814743552 | bytes 31981592 | tf_op jit(solution)/shard_map/nthd,nhde->nthe/dot_general | solution.py:105
  665.2 17.9 %fusion = (f32[24,128]{1,0:T(8,128)S(1)}, f32[24,8,128,128]{3,2,1,0:T(8,128)}) fusion(f32[24,8,128,128]{3,2,1,0:T(8,128)} %fusion.7, bf16[24,128,8,128]{1,3,2,0:T(8,128)(2,1)} %bitcast.61, pred[128,128]{1,0:T(8,128)(4,1)S(1)} %iota_compare_fusion, bf16[24,128,8,128]{1,3,2,0:T(8,128)(2,1)} %bitcast.63, bf16[24,128,8,128]{1,3,2,0:T(8,128)(2,1)} %bitcast.59), kind=kOutput, calls=%fused_computation.12 | convolution fusion | flops 1626338304 | bytes 44068864 | tf_op jit(solution)/shard_map/nhts,nshd->nthd/dot_general | solution.py:101
  683.1 12.6 %copy.67 = f32[24,128,1024]{2,1,0:T(8,128)} copy(f32[24,128,1024]{1,2,0:T(8,128)} %bitcast.64) | data formatting | bytes 25165824 | tf_op jit(solution)/shard_map/reshape | solution.py:109
  695.7 17.0 %psum.7 = f32[3072]{0:T(1024)S(1)} all-reduce(f32[3072]{0:T(1024)S(1)} %bitcast.70), channel_id=1, replica_groups=mesh['seq'=32,'head'=4] {'head'}, use_global_device_ids=true, to_apply=%region_7.10 | all-reduce | flops 3072 | bytes 24576 | tf_op jit(solution)/shard_map/psum | solution.py:112
  712.7 8.3 multiply_convert_fusion
  742.5 124.2 %all-to-all-done.4 = bf16[32,128,1024]{2,1,0:T(8,128)(2,1)} async-done(((bf16[32,128,1024]{2,1,0:T(8,128)(2,1)}), bf16[32,128,1024]{2,1,0:T(8,128)(2,1)}, u32[]{:S(2)}, u32[]{:S(2)}) %all-to-all-start.4) | async-done | bytes 8388640 | tf_op jit(solution)/shard_map/all_to_all | solution.py:141
  866.7 7.9 gather_fusion.8
  (114 shorter events, 129.0 us)
Async XLA Ops:
  9.0 47.5 %all-to-all-start = ((s32[32,1,1]{2,1,0:T(1,128)}), s32[32,1,1]{2,1,0:T(1,128)S(1)}, u32[]{:S(2)}, u32[]{:S(2)}) async-start(s32[32,1,1]{2,1,0:T(1,128)} %copy.55), calls=%async_computation | async-start | bytes 32768 | tf_op jit(solution)/shard_map/all_to_all | solution.py:130
  56.5 102.0 %copy-start = (bf16[32,128,1024]{2,1,0:T(8,128)(2,1)S(1)}, bf16[32,128,1024]{2,1,0:T(8,128)(2,1)}, u32[]{:S(2)}) copy-start(bf16[32,128,1024]{2,1,0:T(8,128)(2,1)} %get-tuple-element.156) | copy-start | bytes 25165828
  257.8 6.3 copy-start.3
  257.8 6.9 copy-start.1
  257.8 130.2 %all-to-all-start.1 = ((bf16[32,128,1024]{2,1,0:T(8,128)(2,1)}), bf16[32,128,1024]{2,1,0:T(8,128)(2,1)}, u32[]{:S(2)}, u32[]{:S(2)}) async-start(bf16[32,128,1024]{2,1,0:T(8,128)(2,1)} %get-tuple-element.154), calls=%async_computation.1 | async-start | bytes 16777216 | tf_op jit(solution)/shard_map/all_to_all | solution.py:129
  264.1 267.1 %all-gather.3.cloned.1.call-start = ((), (), s32[]{:S(2)}) async-start(), calls=%async_computation.5 | async-start | bytes 17301504 | tf_op jit(solution)/shard_map/all_gather | solution.py:13
  683.1 29.6 %copy-start.2 = (f32[1024]{0:T(1024)S(1)}, f32[1024]{0:T(1024)}, u32[]{:S(2)}) copy-start(f32[1024]{0:T(1024)} %param.15) | copy-start | bytes 12292
  736.4 130.4 %all-to-all-start.4 = ((bf16[32,128,1024]{2,1,0:T(8,128)(2,1)}), bf16[32,128,1024]{2,1,0:T(8,128)(2,1)}, u32[]{:S(2)}, u32[]{:S(2)}) async-start(bf16[32,128,1024]{2,1,0:T(8,128)(2,1)} %select_select_fusion.1), calls=%async_computation.4 | async-start | bytes 16777216 | tf_op jit(solution)/shard_map/all_to_all | solution.py:141
Sparse Core Ops, SparseCore 0:
  458.1 72.9 all-gather.2
where the time goes:
time: 896 us; the launch traced here: 888 us
  waiting for transfers between devices  263 us (29%)
  blocking collectives  229 us (26%)
  local copies, waits for them, and re-layouts  123 us (14%)
  other arithmetic  94.7 us (11%)
  matrix products  84.4 us (9%)
  loops' own time  59.1 us (7%)
  starting transfers between devices  19.9 us (2%)
  between operations  13.8 us (2%)
    all_to_all x1, waiting for transfers between devices, on_device(): lax.all_to_all(return_slots(scored_rows, got_labels), 'seq', split_axis=0...  124 us
    all_to_all x1, waiting for transfers between devices, on_device(): lax.all_to_all(value_blocks, 'seq', split_axis=0, concat_axis=0, tiled=True)  106 us
    all_to_all x1, blocking collectives, on_device(): lax.all_to_all(query_blocks, 'seq', split_axis=0, concat_axis=0, tiled=True)  102 us
    all_to_all x1, blocking collectives, on_device(): lax.all_to_all(key_blocks, 'seq', split_axis=0, concat_axis=0, tiled=True)  99.4 us
    another operation x1, loops' own time, prefix(): return lax.fori_loop(0, count - 1, step, subtotal)  59.1 us
    select_n x31, other arithmetic, step(): jnp.where(position < mine, new, old)  40.3 us
    all_gather x1, waiting for transfers between devices, prefix(): pieces = jax.tree.map(lambda part: lax.all_gather(part, axis), value)  33.6 us
    gather x3, local copies, waits for them, and re-layouts, pack_slots(): picked = jnp.take(data, source_index, axis=0)  23.3 us
  transfers between devices with their start and end apart: 4, of which 3 were waited for; matrix products, arithmetic and copies ran while one was open for 10% of the time, Pallas kernels for 0%

commit v1 on v0

v1 whole, which is shorter than its diff:
```python
import jax
import jax.numpy as jnp
from jax import lax
from jax.experimental import pallas as pl
from jax.experimental.pallas import tpu as pltpu
from jax.sharding import PartitionSpec as P

HD = 128
BLOCK = 128
BLOCKS_DEV = 24
HEADS_DEV = 8
SEQ = 32
NBLOCK = SEQ * BLOCKS_DEV
FEATURES = HEADS_DEV * HD
SLICE = FEATURES // SEQ
STEP = 3
MIB = 1 << 20
F32 = jnp.float32
BF16 = jnp.bfloat16


def params(mib):
    return pltpu.CompilerParams(vmem_limit_bytes=mib * MIB)


def head_cols(h):
    return slice(h * HD, (h + 1) * HD)


def block_rows(j):
    return slice(j * BLOCK, (j + 1) * BLOCK)


def states_kernel(k_ref, v_ref, out_ref):
    for j in range(STEP):
        for h in range(HEADS_DEV):
            state = lax.dot_general(
                k_ref[block_rows(j), head_cols(h)],
                v_ref[block_rows(j), head_cols(h)],
                (((0,), (0,)), ((), ())),
                preferred_element_type=F32,
            ).astype(BF16)
            parts = HD // SLICE
            out_ref[h * parts : (h + 1) * parts, j] = state.reshape(parts, SLICE, HD)


def states(keys, values):
    rows = pl.BlockSpec((STEP * BLOCK, FEATURES), lambda i: (i, 0))
    return pl.pallas_call(
        states_kernel,
        grid=(BLOCKS_DEV // STEP,),
        in_specs=[rows, rows],
        out_specs=pl.BlockSpec((SEQ, STEP, SLICE, HD), lambda i: (0, i, 0, 0)),
        out_shape=jax.ShapeDtypeStruct((SEQ, BLOCKS_DEV, SLICE, HD), BF16),
        compiler_params=params(58),
        cost_estimate=pl.CostEstimate(
            flops=2 * BLOCKS_DEV * HEADS_DEV * HD**3, bytes_accessed=18 * MIB, transcendentals=0
        ),
        name="block_states",
    )(keys, values)


def local_kernel(q_ref, k_ref, v_ref, out_ref):
    row = lax.broadcasted_iota(jnp.int32, (BLOCK, BLOCK), 0)
    col = lax.broadcasted_iota(jnp.int32, (BLOCK, BLOCK), 1)
    causal = col <= row
    for j in range(STEP):
        for h in range(HEADS_DEV):
            at = (block_rows(j), head_cols(h))
            scores = lax.dot_general(
                q_ref[at], k_ref[at], (((1,), (1,)), ((), ())), preferred_element_type=F32
            )
            scores = jnp.where(causal, scores, 0.0).astype(BF16)
            out_ref[at] = jnp.dot(scores, v_ref[at], preferred_element_type=F32)


def local_part(queries, keys, values):
    rows = pl.BlockSpec((STEP * BLOCK, FEATURES), lambda i: (i, 0))
    return pl.pallas_call(
        local_kernel,
        grid=(BLOCKS_DEV // STEP,),
        in_specs=[rows, rows, rows],
        out_specs=rows,
        out_shape=jax.ShapeDtypeStruct((BLOCKS_DEV * BLOCK, FEATURES), F32),
        compiler_params=params(58),
        cost_estimate=pl.CostEstimate(
            flops=4 * BLOCKS_DEV * HEADS_DEV * HD**3, bytes_accessed=30 * MIB, transcendentals=0
        ),
        name="local_part",
    )(queries, keys, values)


def prefix_kernel(plan_ref, states_ref, out_ref):
    rows = states_ref.shape[1]

    def step(g, carry):
        total, last = carry
        block = plan_ref[0, g]
        segment = plan_ref[1, g]
        total = jnp.where(segment == last, total, 0.0)
        out_ref[block] = total.astype(BF16)
        return total + states_ref[block].astype(F32), segment

    lax.fori_loop(
        0, NBLOCK, step, (jnp.zeros((rows, HD), F32), jnp.int32(-1)), unroll=4
    )


def prefix(plan, got):
    rows = 16
    part = pl.BlockSpec((NBLOCK, rows, HD), lambda i, plan: (0, i, 0))
    return pl.pallas_call(
        prefix_kernel,
        grid_spec=pltpu.PrefetchScalarGridSpec(
            num_scalar_prefetch=1, grid=(SLICE // rows,), in_specs=[part], out_specs=part
        ),
        out_shape=jax.ShapeDtypeStruct((NBLOCK, SLICE, HD), BF16),
        compiler_params=params(58),
        cost_estimate=pl.CostEstimate(
            flops=NBLOCK * SLICE * HD * 2, bytes_accessed=12 * MIB, transcendentals=0
        ),
        name="prefix",
    )(plan, got)


def cross_kernel(q_ref, local_ref, carried_ref, out_ref, square_ref):
    for j in range(STEP):
        squares = jnp.zeros((BLOCK, HD), F32)
        for h in range(HEADS_DEV):
            at = (block_rows(j), head_cols(h))
            parts = HD // SLICE
            carried = carried_ref[h * parts : (h + 1) * parts, j].reshape(HD, HD)
            attended = local_ref[at] + jnp.dot(q_ref[at], carried, preferred_element_type=F32)
            out_ref[at] = attended
            squares = squares + attended * attended
        square_ref[0, j : j + 1, :] = jnp.sum(squares.T, axis=0, keepdims=True)


def cross_part(queries, local, carried):
    rows = pl.BlockSpec((STEP * BLOCK, FEATURES), lambda i: (i, 0))
    return pl.pallas_call(
        cross_kernel,
        grid=(BLOCKS_DEV // STEP,),
        in_specs=[
            rows,
            rows,
            pl.BlockSpec((SEQ, STEP, SLICE, HD), lambda i: (0, i, 0, 0)),
        ],
        out_specs=[rows, pl.BlockSpec((1, STEP, BLOCK), lambda i: (i, 0, 0))],
        out_shape=[
            jax.ShapeDtypeStruct((BLOCKS_DEV * BLOCK, FEATURES), F32),
            jax.ShapeDtypeStruct((BLOCKS_DEV // STEP, STEP, BLOCK), F32),
        ],
        compiler_params=params(58),
        cost_estimate=pl.CostEstimate(
            flops=2 * BLOCKS_DEV * HEADS_DEV * HD**3, bytes_accessed=36 * MIB, transcendentals=0
        ),
        name="cross_part",
    )(queries, local, carried)


def finish_kernel(width, attended_ref, gain_ref, *refs):
    square_refs, out_ref = refs[:-1], refs[-1]
    total = square_refs[0][0]
    for ref in square_refs[1:]:
        total = total + ref[0]
    scaling = lax.rsqrt(total / width + 1e-05)
    for j in range(STEP):
        factor = jnp.broadcast_to(scaling[j : j + 1, :], (HD, BLOCK)).T
        for h in range(HEADS_DEV):
            at = (block_rows(j), head_cols(h))
            out_ref[at] = (attended_ref[at] * factor * gain_ref[:, head_cols(h)]).astype(BF16)


def finish(attended, gain, squares, width):
    rows = pl.BlockSpec((STEP * BLOCK, FEATURES), lambda i: (i, 0))
    sums = pl.BlockSpec((1, STEP, BLOCK), lambda i: (i, 0, 0))
    return pl.pallas_call(
        lambda *refs: finish_kernel(width, *refs),
        grid=(BLOCKS_DEV // STEP,),
        in_specs=[rows, pl.BlockSpec((1, FEATURES), lambda i: (0, 0))] + [sums] * len(squares),
        out_specs=rows,
        out_shape=jax.ShapeDtypeStruct((BLOCKS_DEV * BLOCK, FEATURES), BF16),
        compiler_params=params(58),
        name="finish_rows",
    )(attended, gain.reshape(1, FEATURES), *squares)


def sequence_plan(placement, segments):
    mine = lax.axis_index("seq")
    positions = jnp.arange(NBLOCK, dtype=jnp.int32)
    loaded = mine * BLOCKS_DEV + jnp.arange(BLOCKS_DEV, dtype=jnp.int32)
    block_at = jnp.sum(
        jnp.where(placement[:, None] == positions[None, :], loaded[:, None], 0), axis=0
    )
    segment_at = jnp.sum(
        jnp.where(loaded[:, None] == positions[None, :], segments[:, None], 0), axis=0
    )
    return lax.psum(jnp.stack([block_at, segment_at]), "seq")


def to_all(value):
    return lax.all_to_all(value, "seq", split_axis=0, concat_axis=0, tiled=True)


def on_device(queries, keys, values, gain, placement, segments):
    head_count = lax.axis_size("head")
    own = states(keys, values)
    got = to_all(own)
    plan = sequence_plan(placement, segments)
    local = local_part(queries, keys, values)
    carried = to_all(
        prefix(plan, got.reshape(NBLOCK, SLICE, HD)).reshape(SEQ, BLOCKS_DEV, SLICE, HD)
    )
    attended, square = cross_part(queries, local, carried)
    squares = [square] + [
        lax.ppermute(square, "head", [(i, (i + s) % head_count) for i in range(head_count)])
        for s in range(1, head_count)
    ]
    return finish(attended, gain, squares, head_count * FEATURES)


def solution(mesh):
    return jax.shard_map(
        on_device,
        mesh=mesh,
        in_specs=(
            P("seq", "head"),
            P("seq", "head"),
            P("seq", "head"),
            P("head"),
            P("seq"),
            P("seq"),
        ),
        out_specs=P("seq", "head"),
        check_vma=False,
    )
```

time: 896 us -> 250 us (0.28)
  waiting for transfers between devices: 263 us -> 58.5 us
  blocking collectives: 229 us -> 88.9 us
  local copies, waits for them, and re-layouts: 123 us -> 0.62 us
  other arithmetic: 94.7 us -> 0.11 us
  matrix products: 84.4 us -> 0 us
  Pallas kernels: 0 us -> 81 us
  loops' own time: 59.1 us -> 0 us
  between operations: 13.8 us -> 0.09 us
    all_to_all x2 -> x0, blocking collectives: 201 us -> none  [the longest x1 102 us: on_device(): lax.all_to_all(query_blocks, 'seq', split_axis=0, concat_axis=0, tiled=True)]
    all_to_all x3 -> x2, waiting for transfers between devices: 230 us -> 54.3 us  [to_all(): return lax.all_to_all(value, 'seq', split_axis=0, concat_axis=0, tiled=True)]
    select_n x41 -> x0, other arithmetic: 85.2 us -> none  [the longest x31 40.3 us: step(): jnp.where(position < mine, new, old)]
    dot_general x5 -> x0, matrix products: 84.4 us -> none  [the longest x1 19.7 us: prefix_states(): jnp.einsum('nm,mhde->nhde', before.astype(jnp.float32), states, precision...]
    pallas_call x0 -> x5, Pallas kernels: none -> 81 us  [the longest x1 33.3 us: local_part(): pl.pallas_call(local_kernel, grid=(BLOCKS_DEV // STEP,), in_specs=[rows,...]
    psum x1, blocking collectives: 17 us -> 88.9 us  [sequence_plan(): return lax.psum(jnp.stack([block_at, segment_at]), 'seq')]
    gather x9 -> x0, local copies, waits for them, and re-layouts: 63.1 us -> none  [the longest x3 23.3 us: pack_slots(): picked = jnp.take(data, source_index, axis=0)]
    another operation x1 -> x0, loops' own time: 59.1 us -> none  [prefix(): return lax.fori_loop(0, count - 1, step, subtotal)]
  transfers between devices with their start and end apart: 4 -> 5, of which waited for: 3 -> 3; matrix products, arithmetic and copies ran while one was open for 10% -> 0% of each run, Pallas kernels for 0% -> 13%
where the time goes in v1:
time: 250 us; the launch traced here: 249 us
  blocking collectives  88.9 us (36%)
  Pallas kernels  81 us (32%)
  waiting for transfers between devices  58.5 us (23%)
  starting transfers between devices  20.1 us (8%)
    psum x1, blocking collectives, sequence_plan(): return lax.psum(jnp.stack([block_at, segment_at]), 'seq')  88.9 us
    all_to_all x2, waiting for transfers between devices, to_all(): return lax.all_to_all(value, 'seq', split_axis=0, concat_axis=0, tiled=True)  54.3 us
    pallas_call x1, Pallas kernels, local_part(): pl.pallas_call(local_kernel, grid=(BLOCKS_DEV // STEP,), in_specs=[rows,...  33.3 us
    all_to_all x2, starting transfers between devices, to_all(): return lax.all_to_all(value, 'seq', split_axis=0, concat_axis=0, tiled=True)  14.9 us
    pallas_call x1, Pallas kernels, cross_part(): pl.pallas_call(cross_kernel, grid=(BLOCKS_DEV // STEP,), in_specs=[rows,...  14.7 us
    pallas_call x1, Pallas kernels, prefix(): pl.pallas_call(prefix_kernel, grid_spec=pltpu.PrefetchScalarGridSpec(num_...  12.4 us
    pallas_call x1, Pallas kernels, states(): pl.pallas_call(states_kernel, grid=(BLOCKS_DEV // STEP,), in_specs=[rows,...  10.3 us
    pallas_call x1, Pallas kernels, finish(): pl.pallas_call(lambda *refs: finish_kernel(width, *refs), grid=(BLOCKS_DE...  10.2 us
  transfers between devices with their start and end apart: 5, of which 3 were waited for; matrix products, arithmetic and copies ran while one was open for 0% of the time, Pallas kernels for 13%

profile of v1, /device:TPU:8, one launch (start us, length us, event | category | flops | bytes accessed | tf_op | source)
XLA Modules:
  0.0 249.4 jit_solution(2926560837858081862)
XLA Ops:
  0.0 10.3 %block_states.1 = bf16[32,24,32,128]{3,2,1,0:T(8,128)(2,1)} custom-call(bf16[3072,1024]{1,0:T(8,128)(2,1)} %k_ref.3, bf16[3072,1024]{1,0:T(8,128)(2,1)} %v_ref.3), custom_call_target="tpu_custom_call" | custom-call | flops 805306368 | bytes 18874368 | tf_op jit(solution)/shard_map/block_states/pallas_call | solution.py:49
  10.3 0.0 copy-start.3
  10.3 0.0 copy-start.4
  10.3 7.7 %all-to-all-start = ((bf16[32,24,32,128]{3,2,1,0:T(8,128)(2,1)}), bf16[32,24,32,128]{3,2,1,0:T(8,128)(2,1)}, u32[]{:S(2)}, u32[]{:S(2)}) async-start(bf16[32,24,32,128]{3,2,1,0:T(8,128)(2,1)} %block_states.1), calls=%async_computation | async-start | bytes 12582912 | tf_op jit(solution)/shard_map/all_to_all | solution.py:203
  18.1 0.0 copy-done.3
  18.1 0.0 copy-done.4
  18.1 0.1 select_reduce_fusion.1
  18.3 88.9 %psum.7.plan_ref = s32[2,768]{1,0:T(2,128)} all-reduce(s32[2,768]{1,0:T(2,128)S(1)} %pad_add_fusion), channel_id=1, replica_groups=mesh['seq'=32,'head'=4] {'seq'}, use_global_device_ids=true, to_apply=%region_2.3 | all-reduce | flops 1536 | bytes 12288 | tf_op jit(solution)/shard_map/psum | solution.py:199
  107.2 0.0 all-to-all-done
  107.2 12.4 %prefix.1 = bf16[768,32,128]{2,1,0:T(8,128)(2,1)} custom-call(s32[2,768]{1,0:T(2,128)} %psum.7.plan_ref, bf16[768,32,128]{2,1,0:T(8,128)(2,1)} %bitcast.states_ref), custom_call_target="tpu_custom_call" | custom-call | flops 6291456 | bytes 12582912 | tf_op jit(solution)/shard_map/prefix/pallas_call | solution.py:112
  119.6 7.1 %all-to-all-start.1 = ((bf16[32,24,32,128]{3,2,1,0:T(8,128)(2,1)}), bf16[32,24,32,128]{3,2,1,0:T(8,128)(2,1)}, u32[]{:S(2)}, u32[]{:S(2)}) async-start(bf16[32,24,32,128]{3,2,1,0:T(8,128)(2,1)} %bitcast.3), calls=%async_computation.1 | async-start | bytes 12582912 | tf_op jit(solution)/shard_map/all_to_all | solution.py:203
  126.8 33.3 %local_part.1.local_ref = f32[3072,1024]{1,0:T(8,128)} custom-call(bf16[3072,1024]{1,0:T(8,128)(2,1)} %q_ref.3, bf16[3072,1024]{1,0:T(8,128)(2,1)} %k_ref.3, bf16[3072,1024]{1,0:T(8,128)(2,1)} %v_ref.3), custom_call_target="tpu_custom_call" | custom-call | flops 1610612736 | bytes 31457280 | tf_op jit(solution)/shard_map/local_part/pallas_call | solution.py:79
  160.1 54.3 %all-to-all-done.1.carried_ref = bf16[32,24,32,128]{3,2,1,0:T(8,128)(2,1)} async-done(((bf16[32,24,32,128]{3,2,1,0:T(8,128)(2,1)}), bf16[32,24,32,128]{3,2,1,0:T(8,128)(2,1)}, u32[]{:S(2)}, u32[]{:S(2)}) %all-to-all-start.1) | async-done | bytes 6291488 | tf_op jit(solution)/shard_map/all_to_all | solution.py:203
  214.4 14.7 %cross_part.1 = (f32[3072,1024]{1,0:T(8,128)}, f32[8,3,128]{2,1,0:T(4,128)}) custom-call(bf16[3072,1024]{1,0:T(8,128)(2,1)} %q_ref.3, f32[3072,1024]{1,0:T(8,128)} %local_part.1.local_ref, bf16[32,24,32,128]{3,2,1,0:T(8,128)(2,1)} %all-to-all-done.1.carried_ref), custom_call_target="tpu_custom_call" | custom-call | flops 805306368 | bytes 37748736 | tf_op jit(solution)/shard_map/cross_part/pallas_call | solution.py:141
  229.1 4.0 %collective-permute-start.2 = (f32[8,3,128]{2,1,0:T(4,128)}, f32[8,3,128]{2,1,0:T(4,128)S(1)}, u32[]{:S(2)}, u32[]{:S(2)}) collective-permute-start(f32[8,3,128]{2,1,0:T(4,128)} %get-tuple-element.8.refs_2_), channel_id=1, source_target_pairs={{0,3},{1,0},{2,1},{3,2},{4,7},{5,4},{6,5},{7,6},{8,11},{9,8},{10,9... | collective-permute-start | bytes 36872 | tf_op jit(solution)/shard_map/ppermute | solution.py:217
  233.1 0.0 collective-permute-start.1
  233.1 1.3 collective-permute-start
  234.4 0.4 collective-permute-done.2.refs_5_
  234.7 3.8 %collective-permute-done.1.refs_4_ = f32[8,3,128]{2,1,0:T(4,128)S(1)} collective-permute-done((f32[8,3,128]{2,1,0:T(4,128)}, f32[8,3,128]{2,1,0:T(4,128)S(1)}, u32[]{:S(2)}, u32[]{:S(2)}) %collective-permute-start.1) | collective-permute-done | bytes 12320 | tf_op jit(solution)/shard_map/ppermute | solution.py:217
  238.5 0.0 collective-permute-done.refs_3_
  238.5 0.0 copy-done
  238.6 0.6 copy-done.1
  239.1 0.0 copy-done.2
  239.2 10.2 %finish_rows.1 = bf16[3072,1024]{1,0:T(8,128)(2,1)} custom-call(f32[3072,1024]{1,0:T(8,128)} %get-tuple-element.7.refs_0_, f32[1,1024]{1,0:T(1,128)} %bitcast.4, f32[8,3,128]{2,1,0:T(4,128)} %get-tuple-element.8.refs_2_, f32[8,3,128]{2,1,0:T(4,128)} %copy-done.2, f32[8,3,128]{2,1,0:T(4,128)} %copy-done.1, f32[8,3,128]{2,1,0:T(4,128)} %copy-done), custom_call_target="tpu_custom_call" | custom-call | tf_op jit(solution)/shard_map/finish_rows/pallas_call | solution.py:178
  (7 shorter events, 0.0 us)
Async XLA Ops:
  10.3 7.8 %copy-start.3 = (s32[24]{0:T(128)S(1)}, s32[24]{0:T(128)}, u32[]{:S(2)}) copy-start(s32[24]{0:T(128)} %param.10) | copy-start | bytes 292
  10.3 7.8 %copy-start.4 = (s32[24]{0:T(128)S(1)}, s32[24]{0:T(128)}, u32[]{:S(2)}) copy-start(s32[24]{0:T(128)} %param.11) | copy-start | bytes 292
  10.3 96.9 %all-to-all-start = ((bf16[32,24,32,128]{3,2,1,0:T(8,128)(2,1)}), bf16[32,24,32,128]{3,2,1,0:T(8,128)(2,1)}, u32[]{:S(2)}, u32[]{:S(2)}) async-start(bf16[32,24,32,128]{3,2,1,0:T(8,128)(2,1)} %block_states.1), calls=%async_computation | async-start | bytes 12582912 | tf_op jit(solution)/shard_map/all_to_all | solution.py:203
  119.6 94.7 %all-to-all-start.1 = ((bf16[32,24,32,128]{3,2,1,0:T(8,128)(2,1)}), bf16[32,24,32,128]{3,2,1,0:T(8,128)(2,1)}, u32[]{:S(2)}, u32[]{:S(2)}) async-start(bf16[32,24,32,128]{3,2,1,0:T(8,128)(2,1)} %bitcast.3), calls=%async_computation.1 | async-start | bytes 12582912 | tf_op jit(solution)/shard_map/all_to_all | solution.py:203
  229.1 5.7 %collective-permute-start.2 = (f32[8,3,128]{2,1,0:T(4,128)}, f32[8,3,128]{2,1,0:T(4,128)S(1)}, u32[]{:S(2)}, u32[]{:S(2)}) collective-permute-start(f32[8,3,128]{2,1,0:T(4,128)} %get-tuple-element.8.refs_2_), channel_id=1, source_target_pairs={{0,3},{1,0},{2,1},{3,2},{4,7},{5,4},{6,5},{7,6},{8,11},{9,8},{10,9... | collective-permute-start | bytes 36872 | tf_op jit(solution)/shard_map/ppermute | solution.py:217
  233.1 5.5 %collective-permute-start.1 = (f32[8,3,128]{2,1,0:T(4,128)}, f32[8,3,128]{2,1,0:T(4,128)S(1)}, u32[]{:S(2)}, u32[]{:S(2)}) collective-permute-start(f32[8,3,128]{2,1,0:T(4,128)} %get-tuple-element.8.refs_2_), channel_id=1, source_target_pairs={{0,2},{1,3},{2,0},{3,1},{4,6},{5,7},{6,4},{7,5},{8,10},{9,11},{10,... | collective-permute-start | bytes 36872 | tf_op jit(solution)/shard_map/ppermute | solution.py:217
  233.1 5.5 %collective-permute-start = (f32[8,3,128]{2,1,0:T(4,128)}, f32[8,3,128]{2,1,0:T(4,128)S(1)}, u32[]{:S(2)}, u32[]{:S(2)}) collective-permute-start(f32[8,3,128]{2,1,0:T(4,128)} %get-tuple-element.8.refs_2_), channel_id=1, source_target_pairs={{0,1},{1,2},{2,3},{3,0},{4,5},{5,6},{6,7},{7,4},{8,9},{9,10},{10,1... | collective-permute-start | bytes 36872 | tf_op jit(solution)/shard_map/ppermute | solution.py:217
  234.7 3.8 %copy-start = (f32[8,3,128]{2,1,0:T(4,128)}, f32[8,3,128]{2,1,0:T(4,128)S(1)}, u32[]{:S(2)}) copy-start(f32[8,3,128]{2,1,0:T(4,128)S(1)} %collective-permute-done.2.refs_5_) | copy-start | bytes 36868
  238.5 0.6 copy-start.1
  238.5 0.6 copy-start.2

commit v2 on v1

v2 whole, which is shorter than its diff:
```python
import jax
import jax.numpy as jnp
from jax import lax
from jax.experimental import pallas as pl
from jax.experimental.pallas import tpu as pltpu
from jax.sharding import PartitionSpec as P

HD = 128
BLOCK = 128
BLOCKS_DEV = 24
HEADS_DEV = 8
SEQ = 32
NBLOCK = SEQ * BLOCKS_DEV
TOKENS_DEV = BLOCKS_DEV * BLOCK
FEATURES = HEADS_DEV * HD
SLICE = FEATURES // SEQ
PARTS = HD // SLICE
SENT = BLOCKS_DEV * SLICE
PLAN = 16
STEP = 4
STEPS = BLOCKS_DEV // STEP
MIB = 1 << 20
F32 = jnp.float32
BF16 = jnp.bfloat16
I32 = jnp.int32
VMEM = pl.BlockSpec(memory_space=pltpu.VMEM)
HBM = pl.BlockSpec(memory_space=pltpu.HBM)


def params(mib):
    return pltpu.CompilerParams(vmem_limit_bytes=mib * MIB)


def head_cols(h):
    return slice(h * HD, (h + 1) * HD)


def rows_at(start, size):
    return pl.ds(pl.multiple_of(start, size), size)


def in_vmem(value):
    return pltpu.with_memory_space_constraint(value, pltpu.VMEM)


def in_hbm(value):
    return pltpu.with_memory_space_constraint(value, pltpu.HBM)


def step_rows(c):
    return rows_at(c * STEP * BLOCK, STEP * BLOCK)


def states_kernel(
    k_ref, v_ref, place_ref, segment_ref, own_ref, k_held, v_held, plan, k_sem, v_sem
):
    def fetch(c, source, target, sem):
        return pltpu.make_async_copy(source.at[step_rows(c)], target.at[step_rows(c)], sem.at[c])

    for c in range(STEPS):
        fetch(c, k_ref, k_held, k_sem).start()
        fetch(c, v_ref, v_held, v_sem).start()
    place = place_ref[...]
    owner = lax.shift_right_logical(place * 2731, 16)
    plan[...] = jnp.zeros_like(plan)
    plan[0:1, 0:BLOCKS_DEV] = owner
    plan[1:2, 0:BLOCKS_DEV] = place - owner * BLOCKS_DEV
    plan[2:3, 0:BLOCKS_DEV] = segment_ref[...]
    own_ref[:, SENT : SENT + PLAN] = jnp.broadcast_to(
        plan[...].astype(F32).astype(BF16)[None], (SEQ, PLAN, HD)
    )

    def step(c, carry):
        fetch(c, k_ref, k_held, k_sem).wait()
        fetch(c, v_ref, v_held, v_sem).wait()
        for j in range(STEP):
            rows = rows_at((c * STEP + j) * BLOCK, BLOCK)
            for h in range(HEADS_DEV):
                state = lax.dot_general(
                    k_held[rows, head_cols(h)],
                    v_held[rows, head_cols(h)],
                    (((0,), (0,)), ((), ())),
                    preferred_element_type=F32,
                ).astype(BF16)
                own_ref[h * PARTS : (h + 1) * PARTS, rows_at((c * STEP + j) * SLICE, SLICE)] = (
                    state.reshape(PARTS, SLICE, HD)
                )
        return carry

    lax.fori_loop(0, STEPS, step, 0)


def states(keys, values, placement, segments):
    held = pltpu.VMEM((TOKENS_DEV, FEATURES), BF16)
    return pl.pallas_call(
        states_kernel,
        in_specs=[HBM, HBM, VMEM, VMEM],
        out_specs=VMEM,
        out_shape=pltpu.VMEM((SEQ, SENT + PLAN, HD), BF16),
        scratch_shapes=[
            held,
            held,
            pltpu.VMEM((PLAN, HD), I32),
            pltpu.SemaphoreType.DMA((STEPS,)),
            pltpu.SemaphoreType.DMA((STEPS,)),
        ],
        compiler_params=params(16),
        name="block_states",
    )(
        in_hbm(keys),
        in_hbm(values),
        placement.reshape(1, BLOCKS_DEV),
        segments.reshape(1, BLOCKS_DEV),
    )


def order_codes(got_ref):
    plan = got_ref[:, SENT : SENT + PLAN].astype(F32)
    owner, within, segment = plan[:, 0, :], plan[:, 1, :], plan[:, 2, :]
    real = lax.broadcasted_iota(I32, (SEQ, HD), 1) < BLOCKS_DEV
    owner = jnp.where(real, owner, -1.0)
    within = jnp.where(real, within, -1.0)
    owner_row = lax.broadcasted_iota(I32, (SEQ, HD), 0).astype(F32)
    within_row = lax.broadcasted_iota(I32, (HD, HD), 0).astype(F32)
    slot = lax.broadcasted_iota(I32, (1, HD), 1).astype(F32)
    picks, spots = [], []
    for d in range(SEQ):
        picks.append(jnp.where(owner[d : d + 1] == owner_row, 1.0, 0.0).astype(BF16))
        here = within[d : d + 1] == within_row[:SEQ]
        spots.append(
            jnp.concatenate(
                [
                    jnp.where(here, float(d), 0.0),
                    jnp.where(here, jnp.broadcast_to(slot, (SEQ, HD)), 0.0),
                    jnp.zeros((HD - 2 * SEQ, HD), F32),
                ],
                axis=0,
            ).astype(BF16)
        )
    table = lax.dot_general(
        jnp.concatenate(picks, axis=1),
        jnp.concatenate(spots, axis=1),
        (((1,), (1,)), ((), ())),
        preferred_element_type=F32,
    )
    loader = table
    slot = jnp.concatenate([table[:, SEQ:], table[:, :SEQ]], axis=1)
    return (
        loader.astype(I32),
        slot.astype(I32),
        segment.astype(I32),
    )


def prefix_kernel(got_ref, out_ref, codes, table, code_sem):
    loader, slot, segment = order_codes(got_ref)
    codes[...] = loader * 32 + slot + segment * 1024
    code_copy = pltpu.make_async_copy(codes, table, code_sem)
    code_copy.start()
    code_copy.wait()

    def owner_step(o, carry):
        total, last = carry
        for w in range(BLOCKS_DEV):
            code = table[o, w]
            loader = lax.shift_right_logical(code, 5) & 31
            slot = code & 31
            segment = lax.shift_right_logical(code, 10)
            at = (loader, rows_at(slot * SLICE, SLICE))
            total = jnp.where(segment == last, total, 0.0)
            out_ref[at] = total.astype(BF16)
            total = total + got_ref[at].astype(F32)
            last = segment
        return total, last

    lax.fori_loop(0, SEQ, owner_step, (jnp.zeros((SLICE, HD), F32), I32(-1)))


def prefix(got):
    return pl.pallas_call(
        prefix_kernel,
        in_specs=[VMEM],
        out_specs=VMEM,
        out_shape=pltpu.VMEM((SEQ, SENT, HD), BF16),
        scratch_shapes=[
            pltpu.VMEM((SEQ, HD), I32),
            pltpu.SMEM((SEQ, HD), I32),
            pltpu.SemaphoreType.DMA,
        ],
        compiler_params=params(8),
        name="prefix",
    )(in_vmem(got))


def attend_kernel(q_ref, k_ref, v_ref, carried_ref, out_ref, square_ref):
    row = lax.broadcasted_iota(I32, (BLOCK, BLOCK), 0)
    col = lax.broadcasted_iota(I32, (BLOCK, BLOCK), 1)
    causal = col <= row

    def step(c, carry):
        for j in range(STEP):
            block = c * STEP + j
            rows = rows_at(block * BLOCK, BLOCK)
            scores = [
                jnp.where(
                    causal,
                    lax.dot_general(
                        q_ref[rows, head_cols(h)],
                        k_ref[rows, head_cols(h)],
                        (((1,), (1,)), ((), ())),
                        preferred_element_type=F32,
                    ),
                    0.0,
                ).astype(BF16)
                for h in range(HEADS_DEV)
            ]
            squares = jnp.zeros((BLOCK, HD), F32)
            for h in range(HEADS_DEV):
                carried = carried_ref[
                    h * PARTS : (h + 1) * PARTS, rows_at(block * SLICE, SLICE)
                ].reshape(HD, HD)
                attended = jnp.dot(
                    jnp.concatenate([scores[h], q_ref[rows, head_cols(h)]], axis=1),
                    jnp.concatenate([v_ref[rows, head_cols(h)], carried], axis=0),
                    preferred_element_type=F32,
                )
                out_ref[rows, head_cols(h)] = attended
                squares = squares + attended * attended
            square_ref[pl.ds(block, 1), :] = jnp.sum(squares.T, axis=0, keepdims=True)
        return carry

    lax.fori_loop(0, STEPS, step, 0)


def attend(queries, keys, values, carried):
    return pl.pallas_call(
        attend_kernel,
        in_specs=[VMEM] * 4,
        out_specs=[VMEM, VMEM],
        out_shape=[
            pltpu.VMEM((TOKENS_DEV, FEATURES), F32),
            jax.ShapeDtypeStruct((BLOCKS_DEV, BLOCK), F32),
        ],
        compiler_params=params(8),
        name="attend",
    )(in_vmem(queries), in_vmem(keys), in_vmem(values), in_vmem(carried))


def finish_kernel(width, attended_ref, gain_ref, *refs):
    square_refs, (out_ref, staged, out_sem) = refs[:-3], refs[-3:]
    total = square_refs[0][...]
    for ref in square_refs[1:]:
        total = total + ref[...]
    scaling = lax.rsqrt(total / width + 1e-05)

    def give(c):
        rows = slice(c * STEP * BLOCK, (c + 1) * STEP * BLOCK)
        return pltpu.make_async_copy(staged.at[rows], out_ref.at[rows], out_sem.at[c])

    for c in range(STEPS):
        for block in range(c * STEP, (c + 1) * STEP):
            rows = slice(block * BLOCK, (block + 1) * BLOCK)
            factor = jnp.broadcast_to(scaling[block : block + 1, :], (HD, BLOCK)).T
            for h in range(HEADS_DEV):
                at = (rows, head_cols(h))
                staged[at] = (attended_ref[at] * factor * gain_ref[:, head_cols(h)]).astype(BF16)
        give(c).start()
    for c in range(STEPS):
        give(c).wait()


def finish(attended, gain, squares, width):
    return pl.pallas_call(
        lambda *refs: finish_kernel(width, *refs),
        in_specs=[VMEM] * (2 + len(squares)),
        out_specs=HBM,
        out_shape=jax.ShapeDtypeStruct((TOKENS_DEV, FEATURES), BF16),
        scratch_shapes=[
            pltpu.VMEM((TOKENS_DEV, FEATURES), BF16),
            pltpu.SemaphoreType.DMA((STEPS,)),
        ],
        compiler_params=params(12),
        name="finish_rows",
    )(in_vmem(attended), gain.reshape(1, FEATURES), *squares)


def to_all(value):
    return lax.all_to_all(value, "seq", split_axis=0, concat_axis=0, tiled=True)


def on_device(queries, keys, values, gain, placement, segments):
    head_count = lax.axis_size("head")
    got = to_all(states(keys, values, placement, segments))
    attended, square = attend(queries, keys, values, to_all(prefix(got)))
    squares = [square] + [
        lax.ppermute(square, "head", [(i, (i + s) % head_count) for i in range(head_count)])
        for s in range(1, head_count)
    ]
    return finish(attended, gain, squares, head_count * FEATURES)


def solution(mesh):
    return jax.shard_map(
        on_device,
        mesh=mesh,
        in_specs=(
            P("seq", "head"),
            P("seq", "head"),
            P("seq", "head"),
            P("head"),
            P("seq"),
            P("seq"),
        ),
        out_specs=P("seq", "head"),
        check_vma=False,
    )
```

time: 250 us -> 194 us (0.78)
  blocking collectives: 88.9 us -> 158 us
  Pallas kernels: 81 us -> 23.5 us
  waiting for transfers between devices: 58.5 us -> 3.94 us
  starting transfers between devices: 20.1 us -> 5.37 us
    all_to_all x0 -> x2, blocking collectives: none -> 158 us  [to_all(): return lax.all_to_all(value, 'seq', split_axis=0, concat_axis=0, tiled=True)]
    psum x1 -> x0, blocking collectives: 88.9 us -> none  [sequence_plan(): return lax.psum(jnp.stack([block_at, segment_at]), 'seq')]
    pallas_call x5 -> x4, Pallas kernels: 81 us -> 23.5 us  [the longest x1 8.69 us: attend(): pl.pallas_call(attend_kernel, in_specs=[VMEM] * 4, out_specs=[VMEM, VMEM]...]
    all_to_all x2 -> x0, waiting for transfers between devices: 54.3 us -> none  [to_all(): return lax.all_to_all(value, 'seq', split_axis=0, concat_axis=0, tiled=True)]
    all_to_all x2 -> x0, starting transfers between devices: 14.9 us -> none  [to_all(): return lax.all_to_all(value, 'seq', split_axis=0, concat_axis=0, tiled=True)]
  transfers between devices with their start and end apart: 5 -> 3, of which waited for: 3 -> 2; matrix products, arithmetic and copies ran while one was open for 0% -> 0% of each run, Pallas kernels for 13% -> 0%
where the time goes in v2:
time: 194 us; the launch traced here: 192 us
  blocking collectives  158 us (81%)
  Pallas kernels  23.5 us (12%)
  starting transfers between devices  5.37 us (3%)
  waiting for transfers between devices  3.94 us (2%)
    all_to_all x2, blocking collectives, to_all(): return lax.all_to_all(value, 'seq', split_axis=0, concat_axis=0, tiled=True)  158 us
    pallas_call x1, Pallas kernels, attend(): pl.pallas_call(attend_kernel, in_specs=[VMEM] * 4, out_specs=[VMEM, VMEM]...  8.69 us
    pallas_call x1, Pallas kernels, prefix(): pl.pallas_call(prefix_kernel, in_specs=[VMEM], out_specs=VMEM, out_shape=...  6.55 us
    ppermute x3, starting transfers between devices, on_device(): lax.ppermute(square, 'head', [(i, (i + s) % head_count) for i in range(he...  5.37 us
    pallas_call x1, Pallas kernels, states(): pl.pallas_call(states_kernel, in_specs=[HBM, HBM, VMEM, VMEM], out_specs=...  5.19 us
    ppermute x3, waiting for transfers between devices, on_device(): lax.ppermute(square, 'head', [(i, (i + s) % head_count) for i in range(he...  3.94 us
  transfers between devices with their start and end apart: 3, of which 2 were waited for; matrix products, arithmetic and copies ran while one was open for 0% of the time, Pallas kernels for 0%

profile of v2, /device:TPU:8, one launch (start us, length us, event | category | flops | bytes accessed | tf_op | source)
XLA Modules:
  0.0 192.2 jit_solution(13812354459151313719)
XLA Ops:
  0.0 0.7 copy-done.1
  0.7 0.7 copy-done.2
  1.3 5.2 %block_states.1 = bf16[32,784,128]{2,1,0:T(8,128)(2,1)S(1)} custom-call(bf16[3072,1024]{1,0:T(8,128)(2,1)} %k_ref.3, bf16[3072,1024]{1,0:T(8,128)(2,1)} %v_ref.3, s32[1,24]{1,0:T(1,128)S(1)} %bitcast.10, s32[1,24]{1,0:T(1,128)S(1)} %bitcast.11), custom_call_target="tpu_custom_call" | custom-call | tf_op jit(solution)/shard_map/block_states/pallas_call | solution.py:95
  6.5 0.0 slice-start
  6.5 0.0 slice-start.2
  6.5 0.0 slice-start.4
  6.5 81.6 %all_to_all.10.got_ref = bf16[32,784,128]{2,1,0:T(8,128)(2,1)S(1)} all-to-all(bf16[32,784,128]{2,1,0:T(8,128)(2,1)S(1)} %block_states.1), channel_id=1, replica_groups=mesh['seq'=32,'head'=4] {'seq'}, dimensions={0} | all-to-all | bytes 12845056 | tf_op jit(solution)/shard_map/all_to_all | solution.py:288
  88.2 6.5 %prefix.1 = bf16[32,768,128]{2,1,0:T(8,128)(2,1)S(1)} custom-call(bf16[32,784,128]{2,1,0:T(8,128)(2,1)S(1)} %all_to_all.10.got_ref), custom_call_target="tpu_custom_call" | custom-call | tf_op jit(solution)/shard_map/prefix/pallas_call | solution.py:180
  94.7 76.4 %all_to_all.11.carried_ref = bf16[32,768,128]{2,1,0:T(8,128)(2,1)S(1)} all-to-all(bf16[32,768,128]{2,1,0:T(8,128)(2,1)S(1)} %prefix.1), channel_id=1, replica_groups=mesh['seq'=32,'head'=4] {'seq'}, dimensions={0} | all-to-all | bytes 12582912 | tf_op jit(solution)/shard_map/all_to_all | solution.py:288
  171.1 0.0 slice-done
  171.1 0.0 slice-done.2
  171.1 0.0 slice-done.1
  171.1 0.0 slice-done.3
  171.1 0.0 slice-done.5
  171.2 0.0 copy-start
  171.2 8.7 %attend.1 = (f32[3072,1024]{1,0:T(8,128)S(1)}, f32[24,128]{1,0:T(8,128)S(1)}) custom-call(bf16[3072,1024]{1,0:T(8,128)(2,1)S(1)} %bitcast.8, bf16[3072,1024]{1,0:T(8,128)(2,1)S(1)} %bitcast.4, bf16[3072,1024]{1,0:T(8,128)(2,1)S(1)} %bitcast.6, bf16[32,768,128]{2,1,0:T(8,128)(2,1)S(1)} %all_to_all.11.carried_ref), custom_call_target="tpu_custom_call" | custom-call | tf_op jit(solution)/shard_map/attend/pallas_call | solution.py:236
  179.9 4.1 %collective-permute-start.2 = (f32[24,128]{1,0:T(8,128)S(1)}, f32[24,128]{1,0:T(8,128)S(1)}, u32[]{:S(2)}, u32[]{:S(2)}) collective-permute-start(f32[24,128]{1,0:T(8,128)S(1)} %get-tuple-element.8.refs_2_), channel_id=1, source_target_pairs={{0,3},{1,0},{2,1},{3,2},{4,7},{5,4},{6,5},{7,6},{8,11},{9,8},{10,9... | collective-permute-start | bytes 36872 | tf_op jit(solution)/shard_map/ppermute | solution.py:296
  184.0 0.0 collective-permute-start.1
  184.0 1.3 collective-permute-start
  185.3 0.1 collective-permute-done.2.refs_5_
  185.4 3.8 %collective-permute-done.1.refs_4_ = f32[24,128]{1,0:T(8,128)S(1)} collective-permute-done((f32[24,128]{1,0:T(8,128)S(1)}, f32[24,128]{1,0:T(8,128)S(1)}, u32[]{:S(2)}, u32[]{:S(2)}) %collective-permute-start.1) | collective-permute-done | bytes 12320 | tf_op jit(solution)/shard_map/ppermute | solution.py:296
  189.2 0.0 collective-permute-done.refs_3_
  189.2 0.0 copy-done
  189.2 3.0 %finish_rows.1 = bf16[3072,1024]{1,0:T(8,128)(2,1)} custom-call(f32[3072,1024]{1,0:T(8,128)S(1)} %get-tuple-element.7.refs_0_, f32[1,1024]{1,0:T(1,128)S(1)} %bitcast.9, f32[24,128]{1,0:T(8,128)S(1)} %get-tuple-element.8.refs_2_, f32[24,128]{1,0:T(8,128)S(1)} %collective-permute-done.refs_3_, f32[24,128]{1,0:T(8,128)S(1)} %collective-permute-done.1.refs_4_, ...), custom_call_target="tpu_custom_call" | custom-call | tf_op jit(solution)/shard_map/finish_rows/pallas_call | solution.py:273
  (9 shorter events, 0.0 us)
Async XLA Ops:
  0.0 0.7 copy-start.1
  0.7 0.7 copy-start.2
  6.5 164.6 %slice-start = ((s8[6291456]{0:T(1024)(128)(4,1)}), s8[4194304]{0:T(1024)(128)(4,1)S(1)}, s32[]{:S(2)}) async-start(s8[6291456]{0:T(1024)(128)(4,1)} %bitcast.3), calls=%async_computation.2 | async-start | bytes 8388608
  6.5 164.6 %slice-start.2 = ((s8[6291456]{0:T(1024)(128)(4,1)}), s8[4194304]{0:T(1024)(128)(4,1)S(1)}, s32[]{:S(2)}) async-start(s8[6291456]{0:T(1024)(128)(4,1)} %bitcast.5), calls=%async_computation.4 | async-start | bytes 8388608
  6.5 164.6 %slice-start.4 = ((s8[6291456]{0:T(1024)(128)(4,1)}), s8[4194304]{0:T(1024)(128)(4,1)S(1)}, s32[]{:S(2)}) async-start(s8[6291456]{0:T(1024)(128)(4,1)} %bitcast.7), calls=%async_computation.6 | async-start | bytes 8388608
  88.2 83.0 %slice-start.1 = ((s8[6291456]{0:T(1024)(128)(4,1)}), s8[2097152]{0:T(1024)(128)(4,1)S(1)}, s32[]{:S(2)}) async-start(s8[6291456]{0:T(1024)(128)(4,1)} %bitcast.3), calls=%async_computation.3 | async-start | bytes 4194304
  88.2 83.0 %slice-start.3 = ((s8[6291456]{0:T(1024)(128)(4,1)}), s8[2097152]{0:T(1024)(128)(4,1)S(1)}, s32[]{:S(2)}) async-start(s8[6291456]{0:T(1024)(128)(4,1)} %bitcast.5), calls=%async_computation.5 | async-start | bytes 4194304
  88.2 83.0 %slice-start.5 = ((s8[6291456]{0:T(1024)(128)(4,1)}), s8[2097152]{0:T(1024)(128)(4,1)S(1)}, s32[]{:S(2)}) async-start(s8[6291456]{0:T(1024)(128)(4,1)} %bitcast.7), calls=%async_computation.7 | async-start | bytes 4194304
  171.2 18.0 %copy-start = (f32[1024]{0:T(1024)S(1)}, f32[1024]{0:T(1024)}, u32[]{:S(2)}) copy-start(f32[1024]{0:T(1024)} %param.9) | copy-start | bytes 12292
  179.9 5.5 %collective-permute-start.2 = (f32[24,128]{1,0:T(8,128)S(1)}, f32[24,128]{1,0:T(8,128)S(1)}, u32[]{:S(2)}, u32[]{:S(2)}) collective-permute-start(f32[24,128]{1,0:T(8,128)S(1)} %get-tuple-element.8.refs_2_), channel_id=1, source_target_pairs={{0,3},{1,0},{2,1},{3,2},{4,7},{5,4},{6,5},{7,6},{8,11},{9,8},{10,9... | collective-permute-start | bytes 36872 | tf_op jit(solution)/shard_map/ppermute | solution.py:296
  184.0 5.2 %collective-permute-start.1 = (f32[24,128]{1,0:T(8,128)S(1)}, f32[24,128]{1,0:T(8,128)S(1)}, u32[]{:S(2)}, u32[]{:S(2)}) collective-permute-start(f32[24,128]{1,0:T(8,128)S(1)} %get-tuple-element.8.refs_2_), channel_id=1, source_target_pairs={{0,2},{1,3},{2,0},{3,1},{4,6},{5,7},{6,4},{7,5},{8,10},{9,11},{10,... | collective-permute-start | bytes 36872 | tf_op jit(solution)/shard_map/ppermute | solution.py:296
  184.0 5.2 %collective-permute-start = (f32[24,128]{1,0:T(8,128)S(1)}, f32[24,128]{1,0:T(8,128)S(1)}, u32[]{:S(2)}, u32[]{:S(2)}) collective-permute-start(f32[24,128]{1,0:T(8,128)S(1)} %get-tuple-element.8.refs_2_), channel_id=1, source_target_pairs={{0,1},{1,2},{2,3},{3,0},{4,5},{5,6},{6,7},{7,4},{8,9},{9,10},{10,1... | collective-permute-start | bytes 36872 | tf_op jit(solution)/shard_map/ppermute | solution.py:296

commit v3 on v2

--- a/solution.py
+++ b/solution.py
@@ -16,9 +16,13 @@
 SLICE = FEATURES // SEQ
 PARTS = HD // SLICE
 SENT = BLOCKS_DEV * SLICE
-PLAN = 16
-STEP = 4
+PLAN = 8
+STEP = 3
 STEPS = BLOCKS_DEV // STEP
+ATTEND_STEP = 24
+GROUP = 24
+OUT_AT = SEQ
+SEGMENT_AT = 2 * SEQ
 MIB = 1 << 20
 F32 = jnp.float32
 BF16 = jnp.bfloat16
@@ -52,23 +56,18 @@
 
 
 def states_kernel(
-    k_ref, v_ref, place_ref, segment_ref, own_ref, k_held, v_held, plan, k_sem, v_sem
+    k_ref, v_ref, place_ref, segment_ref, own_ref, k_held, v_held, given, plan, k_sem, v_sem, sem
 ):
     def fetch(c, source, target, sem):
         return pltpu.make_async_copy(source.at[step_rows(c)], target.at[step_rows(c)], sem.at[c])
 
+    place_copy = pltpu.make_async_copy(place_ref, given.at[0], sem.at[0])
+    segment_copy = pltpu.make_async_copy(segment_ref, given.at[1], sem.at[1])
+    place_copy.start()
+    segment_copy.start()
     for c in range(STEPS):
         fetch(c, k_ref, k_held, k_sem).start()
         fetch(c, v_ref, v_held, v_sem).start()
-    place = place_ref[...]
-    owner = lax.shift_right_logical(place * 2731, 16)
-    plan[...] = jnp.zeros_like(plan)
-    plan[0:1, 0:BLOCKS_DEV] = owner
-    plan[1:2, 0:BLOCKS_DEV] = place - owner * BLOCKS_DEV
-    plan[2:3, 0:BLOCKS_DEV] = segment_ref[...]
-    own_ref[:, SENT : SENT + PLAN] = jnp.broadcast_to(
-        plan[...].astype(F32).astype(BF16)[None], (SEQ, PLAN, HD)
-    )
 
     def step(c, carry):
         fetch(c, k_ref, k_held, k_sem).wait()
@@ -88,90 +87,109 @@
         return carry
 
     lax.fori_loop(0, STEPS, step, 0)
+    place_copy.wait()
+    segment_copy.wait()
+    place = given[0]
+    owner = lax.shift_right_logical(place * 2731, 16)
+    plan[...] = jnp.zeros_like(plan)
+    plan[0:1, 0:BLOCKS_DEV] = owner
+    plan[1:2, 0:BLOCKS_DEV] = place - owner * BLOCKS_DEV
+    plan[2:3, SEGMENT_AT : SEGMENT_AT + BLOCKS_DEV] = given[1]
+    own_ref[:, SENT : SENT + PLAN] = jnp.broadcast_to(
+        plan[...].astype(F32).astype(BF16)[None], (SEQ, PLAN, HD)
+    )
 
 
 def states(keys, values, placement, segments):
     held = pltpu.VMEM((TOKENS_DEV, FEATURES), BF16)
     return pl.pallas_call(
         states_kernel,
-        in_specs=[HBM, HBM, VMEM, VMEM],
+        in_specs=[HBM] * 4,
         out_specs=VMEM,
         out_shape=pltpu.VMEM((SEQ, SENT + PLAN, HD), BF16),
         scratch_shapes=[
             held,
             held,
+            pltpu.VMEM((2, 1, BLOCKS_DEV), I32),
             pltpu.VMEM((PLAN, HD), I32),
             pltpu.SemaphoreType.DMA((STEPS,)),
             pltpu.SemaphoreType.DMA((STEPS,)),
+            pltpu.SemaphoreType.DMA((2,)),
         ],
         compiler_params=params(16),
         name="block_states",
     )(
         in_hbm(keys),
         in_hbm(values),
-        placement.reshape(1, BLOCKS_DEV),
-        segments.reshape(1, BLOCKS_DEV),
+        in_hbm(placement.reshape(1, BLOCKS_DEV)),
+        in_hbm(segments.reshape(1, BLOCKS_DEV)),
     )
 
 
-def order_codes(got_ref):
+def block_order(got_ref):
     plan = got_ref[:, SENT : SENT + PLAN].astype(F32)
-    owner, within, segment = plan[:, 0, :], plan[:, 1, :], plan[:, 2, :]
-    real = lax.broadcasted_iota(I32, (SEQ, HD), 1) < BLOCKS_DEV
-    owner = jnp.where(real, owner, -1.0)
-    within = jnp.where(real, within, -1.0)
-    owner_row = lax.broadcasted_iota(I32, (SEQ, HD), 0).astype(F32)
-    within_row = lax.broadcasted_iota(I32, (HD, HD), 0).astype(F32)
-    slot = lax.broadcasted_iota(I32, (1, HD), 1).astype(F32)
+    spot_row = lax.broadcasted_iota(I32, (SEQ, HD), 0).astype(F32)
+    lane = lax.broadcasted_iota(I32, (SEQ, HD), 1)
+    slot = lane.astype(F32)
+    real = lane < BLOCKS_DEV
+    owner_row = jnp.where(real, spot_row, -1.0)
     picks, spots = [], []
     for d in range(SEQ):
-        picks.append(jnp.where(owner[d : d + 1] == owner_row, 1.0, 0.0).astype(BF16))
-        here = within[d : d + 1] == within_row[:SEQ]
+        picks.append(jnp.where(plan[d, 0:1] == owner_row, 1.0, 0.0).astype(BF16))
+        here = plan[d, 1:2] == spot_row
         spots.append(
             jnp.concatenate(
-                [
-                    jnp.where(here, float(d), 0.0),
-                    jnp.where(here, jnp.broadcast_to(slot, (SEQ, HD)), 0.0),
-                    jnp.zeros((HD - 2 * SEQ, HD), F32),
-                ],
-                axis=0,
+                [jnp.where(here, float(d), 0.0), jnp.where(here, slot, 0.0)], axis=0
             ).astype(BF16)
         )
-    table = lax.dot_general(
+    found = lax.dot_general(
         jnp.concatenate(picks, axis=1),
         jnp.concatenate(spots, axis=1),
         (((1,), (1,)), ((), ())),
         preferred_element_type=F32,
-    )
-    loader = table
-    slot = jnp.concatenate([table[:, SEQ:], table[:, :SEQ]], axis=1)
-    return (
-        loader.astype(I32),
-        slot.astype(I32),
-        segment.astype(I32),
-    )
-
-
-def prefix_kernel(got_ref, out_ref, codes, table, code_sem):
-    loader, slot, segment = order_codes(got_ref)
-    codes[...] = loader * 32 + slot + segment * 1024
-    code_copy = pltpu.make_async_copy(codes, table, code_sem)
-    code_copy.start()
-    code_copy.wait()
+    ).astype(I32)
+    loader, slot = found[:, :SEQ], found[:, SEQ:]
+    got_at = loader * (SENT + PLAN) + slot * SLICE
+    out_at = loader * SENT + slot * SLICE
+    rows = jnp.concatenate([got_at, out_at, jnp.zeros((SEQ, HD - 2 * SEQ), I32)], axis=1)
+    return jnp.where(lane < SEGMENT_AT, rows, plan[:, 2, :].astype(I32))
+
+
+def prefix_kernel(got_ref, out_ref, order, table, order_sem):
+    order[...] = block_order(got_ref)
+    order_copy = pltpu.make_async_copy(order, table, order_sem)
+    order_copy.start()
+    order_copy.wait()
+    got_rows = got_ref.reshape(SEQ * (SENT + PLAN), HD)
+    out_rows = out_ref.reshape(SEQ * SENT, HD)
 
     def owner_step(o, carry):
-        total, last = carry
-        for w in range(BLOCKS_DEV):
-            code = table[o, w]
-            loader = lax.shift_right_logical(code, 5) & 31
-            slot = code & 31
-            segment = lax.shift_right_logical(code, 10)
-            at = (loader, rows_at(slot * SLICE, SLICE))
-            total = jnp.where(segment == last, total, 0.0)
-            out_ref[at] = total.astype(BF16)
-            total = total + got_ref[at].astype(F32)
-            last = segment
-        return total, last
+        for first in range(0, BLOCKS_DEV, GROUP):
+            group = range(first, first + GROUP)
+
+            def run(total, last, check):
+                loaded = [got_rows[rows_at(table[o, w], SLICE), :] for w in group]
+                before = []
+                for w, state in zip(group, loaded):
+                    if check:
+                        segment = table[o, SEGMENT_AT + w]
+                        total = jnp.where(segment == last, total, 0.0)
+                        last = segment
+                    before.append(total.astype(BF16))
+                    total = total + state.astype(F32)
+                for w, value in zip(group, before):
+                    out_rows[rows_at(table[o, OUT_AT + w], SLICE), :] = value
+                return total, last
+
+            total, last = carry
+            carry = lax.cond(
+                table[o, SEGMENT_AT + group[-1]] == last,
+                lambda total, last: run(total, last, False),
+                lambda total, last: run(total, last, True),
+                total,
+                last,
+            )
+        return carry
 
     lax.fori_loop(0, SEQ, owner_step, (jnp.zeros((SLICE, HD), F32), I32(-1)))
 
@@ -198,8 +216,8 @@
     causal = col <= row
 
     def step(c, carry):
-        for j in range(STEP):
-            block = c * STEP + j
+        for j in range(ATTEND_STEP):
+            block = c * ATTEND_STEP + j
             rows = rows_at(block * BLOCK, BLOCK)
             scores = [
                 jnp.where(
@@ -229,7 +247,7 @@
             square_ref[pl.ds(block, 1), :] = jnp.sum(squares.T, axis=0, keepdims=True)
         return carry
 
-    lax.fori_loop(0, STEPS, step, 0)
+    lax.fori_loop(0, BLOCKS_DEV // ATTEND_STEP, step, 0)
 
 
 def attend(queries, keys, values, carried):

time: 194 us -> 188 us (0.969)
  Pallas kernels: 23.5 us -> 20 us
    pallas_call x1, Pallas kernels: 6.55 us -> 4.12 us  [prefix(): pl.pallas_call(prefix_kernel, in_specs=[VMEM], out_specs=VMEM, out_shape=...]
where the time goes in v3:
time: 188 us; the launch traced here: 187 us
  blocking collectives  157 us (84%)
  Pallas kernels  20 us (11%)
  starting transfers between devices  5.4 us (3%)
  waiting for transfers between devices  3.93 us (2%)
    all_to_all x2, blocking collectives, to_all(): return lax.all_to_all(value, 'seq', split_axis=0, concat_axis=0, tiled=True)  157 us
    pallas_call x1, Pallas kernels, attend(): pl.pallas_call(attend_kernel, in_specs=[VMEM] * 4, out_specs=[VMEM, VMEM]...  7.63 us
    ppermute x3, starting transfers between devices, on_device(): lax.ppermute(square, 'head', [(i, (i + s) % head_count) for i in range(he...  5.4 us
    pallas_call x1, Pallas kernels, states(): pl.pallas_call(states_kernel, in_specs=[HBM] * 4, out_specs=VMEM, out_sha...  5.25 us
    pallas_call x1, Pallas kernels, prefix(): pl.pallas_call(prefix_kernel, in_specs=[VMEM], out_specs=VMEM, out_shape=...  4.12 us
    ppermute x3, waiting for transfers between devices, on_device(): lax.ppermute(square, 'head', [(i, (i + s) % head_count) for i in range(he...  3.93 us
  transfers between devices with their start and end apart: 3, of which 2 were waited for; matrix products, arithmetic and copies ran while one was open for 0% of the time, Pallas kernels for 0%

profile of v3, /device:TPU:8, one launch (start us, length us, event | category | flops | bytes accessed | tf_op | source)
XLA Modules:
  0.0 186.9 jit_solution(15646886027125771572)
XLA Ops:
  0.0 5.3 %block_states.1 = bf16[32,776,128]{2,1,0:T(8,128)(2,1)S(1)} custom-call(bf16[3072,1024]{1,0:T(8,128)(2,1)} %k_ref.3, bf16[3072,1024]{1,0:T(8,128)(2,1)} %v_ref.3, s32[1,24]{1,0:T(1,128)} %bitcast.10, s32[1,24]{1,0:T(1,128)} %bitcast.11), custom_call_target="tpu_custom_call" | custom-call | tf_op jit(solution)/shard_map/block_states/pallas_call | solution.py:105
  5.3 0.0 slice-start
  5.3 0.0 slice-start.2
  5.3 0.0 slice-start.4
  5.3 81.1 %all_to_all.10.got_ref = bf16[32,776,128]{2,1,0:T(8,128)(2,1)S(1)} all-to-all(bf16[32,776,128]{2,1,0:T(8,128)(2,1)S(1)} %block_states.1), channel_id=1, replica_groups=mesh['seq'=32,'head'=4] {'seq'}, dimensions={0} | all-to-all | bytes 12713984 | tf_op jit(solution)/shard_map/all_to_all | solution.py:306
  86.4 0.0 slice-start.1
  86.4 4.1 %prefix.1 = bf16[32,768,128]{2,1,0:T(8,128)(2,1)S(1)} custom-call(bf16[32,776,128]{2,1,0:T(8,128)(2,1)S(1)} %all_to_all.10.got_ref), custom_call_target="tpu_custom_call" | custom-call | tf_op jit(solution)/shard_map/prefix/pallas_call | solution.py:198
  90.5 76.3 %all_to_all.11.carried_ref = bf16[32,768,128]{2,1,0:T(8,128)(2,1)S(1)} all-to-all(bf16[32,768,128]{2,1,0:T(8,128)(2,1)S(1)} %prefix.1), channel_id=1, replica_groups=mesh['seq'=32,'head'=4] {'seq'}, dimensions={0} | all-to-all | bytes 12582912 | tf_op jit(solution)/shard_map/all_to_all | solution.py:306
  166.8 0.0 slice-done
  166.8 0.0 slice-done.2
  166.9 0.0 slice-done.4
  166.9 0.0 slice-done.1
  166.9 0.0 slice-done.3
  166.9 0.0 slice-done.5
  166.9 0.0 copy-start
  166.9 7.6 %attend.1 = (f32[3072,1024]{1,0:T(8,128)S(1)}, f32[24,128]{1,0:T(8,128)S(1)}) custom-call(bf16[3072,1024]{1,0:T(8,128)(2,1)S(1)} %bitcast.8, bf16[3072,1024]{1,0:T(8,128)(2,1)S(1)} %bitcast.4, bf16[3072,1024]{1,0:T(8,128)(2,1)S(1)} %bitcast.6, bf16[32,768,128]{2,1,0:T(8,128)(2,1)S(1)} %all_to_all.11.carried_ref), custom_call_target="tpu_custom_call" | custom-call | tf_op jit(solution)/shard_map/attend/pallas_call | solution.py:254
  174.6 4.1 %collective-permute-start.2 = (f32[24,128]{1,0:T(8,128)S(1)}, f32[24,128]{1,0:T(8,128)S(1)}, u32[]{:S(2)}, u32[]{:S(2)}) collective-permute-start(f32[24,128]{1,0:T(8,128)S(1)} %get-tuple-element.8.refs_2_), channel_id=1, source_target_pairs={{0,3},{1,0},{2,1},{3,2},{4,7},{5,4},{6,5},{7,6},{8,11},{9,8},{10,9... | collective-permute-start | bytes 36872 | tf_op jit(solution)/shard_map/ppermute | solution.py:314
  178.7 0.0 collective-permute-start.1
  178.7 1.3 collective-permute-start
  180.0 0.1 collective-permute-done.2.refs_5_
  180.1 3.8 %collective-permute-done.1.refs_4_ = f32[24,128]{1,0:T(8,128)S(1)} collective-permute-done((f32[24,128]{1,0:T(8,128)S(1)}, f32[24,128]{1,0:T(8,128)S(1)}, u32[]{:S(2)}, u32[]{:S(2)}) %collective-permute-start.1) | collective-permute-done | bytes 12320 | tf_op jit(solution)/shard_map/ppermute | solution.py:314
  183.9 0.0 collective-permute-done.refs_3_
  183.9 0.0 copy-done
  183.9 3.0 %finish_rows.1 = bf16[3072,1024]{1,0:T(8,128)(2,1)} custom-call(f32[3072,1024]{1,0:T(8,128)S(1)} %get-tuple-element.7.refs_0_, f32[1,1024]{1,0:T(1,128)S(1)} %bitcast.9, f32[24,128]{1,0:T(8,128)S(1)} %get-tuple-element.8.refs_2_, f32[24,128]{1,0:T(8,128)S(1)} %collective-permute-done.refs_3_, f32[24,128]{1,0:T(8,128)S(1)} %collective-permute-done.1.refs_4_, ...), custom_call_target="tpu_custom_call" | custom-call | tf_op jit(solution)/shard_map/finish_rows/pallas_call | solution.py:291
  (5 shorter events, 0.0 us)
Async XLA Ops:
  5.3 161.6 %slice-start = ((s8[6291456]{0:T(1024)(128)(4,1)}), s8[4194304]{0:T(1024)(128)(4,1)S(1)}, s32[]{:S(2)}) async-start(s8[6291456]{0:T(1024)(128)(4,1)} %bitcast.3), calls=%async_computation.2 | async-start | bytes 8388608
  5.3 161.6 %slice-start.2 = ((s8[6291456]{0:T(1024)(128)(4,1)}), s8[4194304]{0:T(1024)(128)(4,1)S(1)}, s32[]{:S(2)}) async-start(s8[6291456]{0:T(1024)(128)(4,1)} %bitcast.5), calls=%async_computation.4 | async-start | bytes 8388608
  5.3 161.6 %slice-start.4 = ((s8[6291456]{0:T(1024)(128)(4,1)}), s8[4194304]{0:T(1024)(128)(4,1)S(1)}, s32[]{:S(2)}) async-start(s8[6291456]{0:T(1024)(128)(4,1)} %bitcast.7), calls=%async_computation.6 | async-start | bytes 8388608
  86.4 80.5 %slice-start.1 = ((s8[6291456]{0:T(1024)(128)(4,1)}), s8[2097152]{0:T(1024)(128)(4,1)S(1)}, s32[]{:S(2)}) async-start(s8[6291456]{0:T(1024)(128)(4,1)} %bitcast.3), calls=%async_computation.3 | async-start | bytes 4194304
  86.4 80.5 %slice-start.3 = ((s8[6291456]{0:T(1024)(128)(4,1)}), s8[2097152]{0:T(1024)(128)(4,1)S(1)}, s32[]{:S(2)}) async-start(s8[6291456]{0:T(1024)(128)(4,1)} %bitcast.5), calls=%async_computation.5 | async-start | bytes 4194304
  86.4 80.5 %slice-start.5 = ((s8[6291456]{0:T(1024)(128)(4,1)}), s8[2097152]{0:T(1024)(128)(4,1)S(1)}, s32[]{:S(2)}) async-start(s8[6291456]{0:T(1024)(128)(4,1)} %bitcast.7), calls=%async_computation.7 | async-start | bytes 4194304
  166.9 17.0 %copy-start = (f32[1024]{0:T(1024)S(1)}, f32[1024]{0:T(1024)}, u32[]{:S(2)}) copy-start(f32[1024]{0:T(1024)} %param.9) | copy-start | bytes 12292
  174.6 5.5 %collective-permute-start.2 = (f32[24,128]{1,0:T(8,128)S(1)}, f32[24,128]{1,0:T(8,128)S(1)}, u32[]{:S(2)}, u32[]{:S(2)}) collective-permute-start(f32[24,128]{1,0:T(8,128)S(1)} %get-tuple-element.8.refs_2_), channel_id=1, source_target_pairs={{0,3},{1,0},{2,1},{3,2},{4,7},{5,4},{6,5},{7,6},{8,11},{9,8},{10,9... | collective-permute-start | bytes 36872 | tf_op jit(solution)/shard_map/ppermute | solution.py:314
  178.7 5.2 %collective-permute-start.1 = (f32[24,128]{1,0:T(8,128)S(1)}, f32[24,128]{1,0:T(8,128)S(1)}, u32[]{:S(2)}, u32[]{:S(2)}) collective-permute-start(f32[24,128]{1,0:T(8,128)S(1)} %get-tuple-element.8.refs_2_), channel_id=1, source_target_pairs={{0,2},{1,3},{2,0},{3,1},{4,6},{5,7},{6,4},{7,5},{8,10},{9,11},{10,... | collective-permute-start | bytes 36872 | tf_op jit(solution)/shard_map/ppermute | solution.py:314
  178.7 5.2 %collective-permute-start = (f32[24,128]{1,0:T(8,128)S(1)}, f32[24,128]{1,0:T(8,128)S(1)}, u32[]{:S(2)}, u32[]{:S(2)}) collective-permute-start(f32[24,128]{1,0:T(8,128)S(1)} %get-tuple-element.8.refs_2_), channel_id=1, source_target_pairs={{0,1},{1,2},{2,3},{3,0},{4,5},{5,6},{6,7},{7,4},{8,9},{9,10},{10,1... | collective-permute-start | bytes 36872 | tf_op jit(solution)/shard_map/ppermute | solution.py:314

commit v4 on v3

--- a/solution.py
+++ b/solution.py
@@ -56,11 +56,15 @@
 
 
 def states_kernel(
-    k_ref, v_ref, place_ref, segment_ref, own_ref, k_held, v_held, given, plan, k_sem, v_sem, sem
+    q_ref, k_ref, v_ref, place_ref, segment_ref, own_ref, scores_ref, q_held, k_held, v_held, given,
+    plan, q_sem, k_sem, v_sem, sem
 ):
     def fetch(c, source, target, sem):
         return pltpu.make_async_copy(source.at[step_rows(c)], target.at[step_rows(c)], sem.at[c])
 
+    row = lax.broadcasted_iota(I32, (BLOCK, BLOCK), 0)
+    col = lax.broadcasted_iota(I32, (BLOCK, BLOCK), 1)
+    causal = col <= row
     place_copy = pltpu.make_async_copy(place_ref, given.at[0], sem.at[0])
     segment_copy = pltpu.make_async_copy(segment_ref, given.at[1], sem.at[1])
     place_copy.start()
@@ -68,22 +72,23 @@
     for c in range(STEPS):
         fetch(c, k_ref, k_held, k_sem).start()
         fetch(c, v_ref, v_held, v_sem).start()
+        fetch(c, q_ref, q_held, q_sem).start()
 
     def step(c, carry):
         fetch(c, k_ref, k_held, k_sem).wait()
         fetch(c, v_ref, v_held, v_sem).wait()
+        fetch(c, q_ref, q_held, q_sem).wait()
         for j in range(STEP):
-            rows = rows_at((c * STEP + j) * BLOCK, BLOCK)
+            block = c * STEP + j
+            rows = rows_at(block * BLOCK, BLOCK)
             for h in range(HEADS_DEV):
-                state = lax.dot_general(
-                    k_held[rows, head_cols(h)],
-                    v_held[rows, head_cols(h)],
-                    (((0,), (0,)), ((), ())),
-                    preferred_element_type=F32,
-                ).astype(BF16)
-                own_ref[h * PARTS : (h + 1) * PARTS, rows_at((c * STEP + j) * SLICE, SLICE)] = (
-                    state.reshape(PARTS, SLICE, HD)
+                turned = k_held[rows, head_cols(h)].T
+                state = jnp.dot(turned, v_held[rows, head_cols(h)], preferred_element_type=F32)
+                own_ref[h * PARTS : (h + 1) * PARTS, rows_at(block * SLICE, SLICE)] = (
+                    state.astype(BF16).reshape(PARTS, SLICE, HD)
                 )
+                scores = jnp.dot(q_held[rows, head_cols(h)], turned, preferred_element_type=F32)
+                scores_ref[rows, head_cols(h)] = jnp.where(causal, scores, 0.0).astype(BF16)
         return carry
 
     lax.fori_loop(0, STEPS, step, 0)
@@ -100,25 +105,28 @@
     )
 
 
-def states(keys, values, placement, segments):
+def states(queries, keys, values, placement, segments):
     held = pltpu.VMEM((TOKENS_DEV, FEATURES), BF16)
     return pl.pallas_call(
         states_kernel,
-        in_specs=[HBM] * 4,
-        out_specs=VMEM,
-        out_shape=pltpu.VMEM((SEQ, SENT + PLAN, HD), BF16),
+        in_specs=[HBM] * 5,
+        out_specs=[VMEM, VMEM],
+        out_shape=[pltpu.VMEM((SEQ, SENT + PLAN, HD), BF16), held],
         scratch_shapes=[
+            held,
             held,
             held,
             pltpu.VMEM((2, 1, BLOCKS_DEV), I32),
             pltpu.VMEM((PLAN, HD), I32),
             pltpu.SemaphoreType.DMA((STEPS,)),
             pltpu.SemaphoreType.DMA((STEPS,)),
+            pltpu.SemaphoreType.DMA((STEPS,)),
             pltpu.SemaphoreType.DMA((2,)),
         ],
-        compiler_params=params(16),
+        compiler_params=params(22),
         name="block_states",
     )(
+        in_hbm(queries),
         in_hbm(keys),
         in_hbm(values),
         in_hbm(placement.reshape(1, BLOCKS_DEV)),
@@ -210,35 +218,20 @@
     )(in_vmem(got))
 
 
-def attend_kernel(q_ref, k_ref, v_ref, carried_ref, out_ref, square_ref):
-    row = lax.broadcasted_iota(I32, (BLOCK, BLOCK), 0)
-    col = lax.broadcasted_iota(I32, (BLOCK, BLOCK), 1)
-    causal = col <= row
-
+def attend_kernel(q_ref, scores_ref, v_ref, carried_ref, out_ref, square_ref):
     def step(c, carry):
         for j in range(ATTEND_STEP):
             block = c * ATTEND_STEP + j
             rows = rows_at(block * BLOCK, BLOCK)
-            scores = [
-                jnp.where(
-                    causal,
-                    lax.dot_general(
-                        q_ref[rows, head_cols(h)],
-                        k_ref[rows, head_cols(h)],
-                        (((1,), (1,)), ((), ())),
-                        preferred_element_type=F32,
-                    ),
-                    0.0,
-                ).astype(BF16)
-                for h in range(HEADS_DEV)
-            ]
             squares = jnp.zeros((BLOCK, HD), F32)
             for h in range(HEADS_DEV):
                 carried = carried_ref[
                     h * PARTS : (h + 1) * PARTS, rows_at(block * SLICE, SLICE)
                 ].reshape(HD, HD)
                 attended = jnp.dot(
-                    jnp.concatenate([scores[h], q_ref[rows, head_cols(h)]], axis=1),
+                    jnp.concatenate(
+                        [scores_ref[rows, head_cols(h)], q_ref[rows, head_cols(h)]], axis=1
+                    ),
                     jnp.concatenate([v_ref[rows, head_cols(h)], carried], axis=0),
                     preferred_element_type=F32,
                 )
@@ -250,7 +243,7 @@
     lax.fori_loop(0, BLOCKS_DEV // ATTEND_STEP, step, 0)
 
 
-def attend(queries, keys, values, carried):
+def attend(queries, scores, values, carried):
     return pl.pallas_call(
         attend_kernel,
         in_specs=[VMEM] * 4,
@@ -261,7 +254,7 @@
         ],
         compiler_params=params(8),
         name="attend",
-    )(in_vmem(queries), in_vmem(keys), in_vmem(values), in_vmem(carried))
+    )(in_vmem(queries), in_vmem(scores), in_vmem(values), in_vmem(carried))
 
 
 def finish_kernel(width, attended_ref, gain_ref, *refs):
@@ -308,8 +301,8 @@
 
 def on_device(queries, keys, values, gain, placement, segments):
     head_count = lax.axis_size("head")
-    got = to_all(states(keys, values, placement, segments))
-    attended, square = attend(queries, keys, values, to_all(prefix(got)))
+    own, scores = states(queries, keys, values, placement, segments)
+    attended, square = attend(queries, scores, values, to_all(prefix(to_all(own))))
     squares = [square] + [
         lax.ppermute(square, "head", [(i, (i + s) % head_count) for i in range(head_count)])
         for s in range(1, head_count)

time: 188 us -> 186 us (0.989)
    pallas_call x1, Pallas kernels: 7.63 us -> 3.77 us  [attend(): pl.pallas_call(attend_kernel, in_specs=[VMEM] * 4, out_specs=[VMEM, VMEM]...]
    pallas_call x1, Pallas kernels: 5.25 us -> 7.31 us  [states(): pl.pallas_call(states_kernel, in_specs=[HBM] * 5, out_specs=[VMEM, VMEM],...]
where the time goes in v4:
time: 186 us; the launch traced here: 185 us
  blocking collectives  157 us (84%)
  Pallas kernels  18.3 us (10%)
  starting transfers between devices  5.37 us (3%)
  waiting for transfers between devices  3.94 us (2%)
    all_to_all x2, blocking collectives, to_all(): return lax.all_to_all(value, 'seq', split_axis=0, concat_axis=0, tiled=True)  157 us
    pallas_call x1, Pallas kernels, states(): pl.pallas_call(states_kernel, in_specs=[HBM] * 5, out_specs=[VMEM, VMEM],...  7.31 us
    ppermute x3, starting transfers between devices, on_device(): lax.ppermute(square, 'head', [(i, (i + s) % head_count) for i in range(he...  5.37 us
    pallas_call x1, Pallas kernels, prefix(): pl.pallas_call(prefix_kernel, in_specs=[VMEM], out_specs=VMEM, out_shape=...  4.19 us
    ppermute x3, waiting for transfers between devices, on_device(): lax.ppermute(square, 'head', [(i, (i + s) % head_count) for i in range(he...  3.94 us
    pallas_call x1, Pallas kernels, attend(): pl.pallas_call(attend_kernel, in_specs=[VMEM] * 4, out_specs=[VMEM, VMEM]...  3.77 us
  transfers between devices with their start and end apart: 3, of which 2 were waited for; matrix products, arithmetic and copies ran while one was open for 0% of the time, Pallas kernels for 0%

profile of v4, /device:TPU:8, one launch (start us, length us, event | category | flops | bytes accessed | tf_op | source)
XLA Modules:
  0.0 185.1 jit_solution(11036617116055064021)
XLA Ops:
  0.0 7.3 %block_states.1 = (bf16[32,776,128]{2,1,0:T(8,128)(2,1)S(1)}, bf16[3072,1024]{1,0:T(8,128)(2,1)S(1)}) custom-call(bf16[3072,1024]{1,0:T(8,128)(2,1)} %q_ref.3, bf16[3072,1024]{1,0:T(8,128)(2,1)} %k_ref.1, bf16[3072,1024]{1,0:T(8,128)(2,1)} %v_ref.3, s32[1,24]{1,0:T(1,128)} %bitcast.8, s32[1,24]{1,0:T(1,128)} %bitcast.9), custom_call_target="tpu_custom_call" | custom-call | tf_op jit(solution)/shard_map/block_states/pallas_call | solution.py:110
  7.3 0.0 slice-start
  7.3 0.0 slice-start.2
  7.3 81.1 %all_to_all.10.got_ref = bf16[32,776,128]{2,1,0:T(8,128)(2,1)S(1)} all-to-all(bf16[32,776,128]{2,1,0:T(8,128)(2,1)S(1)} %get-tuple-element.10), channel_id=1, replica_groups=mesh['seq'=32,'head'=4] {'seq'}, dimensions={0} | all-to-all | bytes 12713984 | tf_op jit(solution)/shard_map/all_to_all | solution.py:299
  88.5 0.0 slice-start.1
  88.5 0.0 slice-start.3
  88.5 4.2 %prefix.1 = bf16[32,768,128]{2,1,0:T(8,128)(2,1)S(1)} custom-call(bf16[32,776,128]{2,1,0:T(8,128)(2,1)S(1)} %all_to_all.10.got_ref), custom_call_target="tpu_custom_call" | custom-call | tf_op jit(solution)/shard_map/prefix/pallas_call | solution.py:206
  92.7 76.3 %all_to_all.11.carried_ref = bf16[32,768,128]{2,1,0:T(8,128)(2,1)S(1)} all-to-all(bf16[32,768,128]{2,1,0:T(8,128)(2,1)S(1)} %prefix.1), channel_id=1, replica_groups=mesh['seq'=32,'head'=4] {'seq'}, dimensions={0} | all-to-all | bytes 12582912 | tf_op jit(solution)/shard_map/all_to_all | solution.py:299
  169.0 0.0 slice-done
  169.0 0.0 slice-done.2
  169.0 0.0 slice-done.1
  169.0 0.0 slice-done.3
  169.0 0.0 copy-start
  169.0 3.8 %attend.1 = (f32[3072,1024]{1,0:T(8,128)S(1)}, f32[24,128]{1,0:T(8,128)S(1)}) custom-call(bf16[3072,1024]{1,0:T(8,128)(2,1)S(1)} %bitcast.4, bf16[3072,1024]{1,0:T(8,128)(2,1)S(1)} %get-tuple-element.9.scores_ref, bf16[3072,1024]{1,0:T(8,128)(2,1)S(1)} %bitcast.6, bf16[32,768,128]{2,1,0:T(8,128)(2,1)S(1)} %all_to_all.11.carried_ref), custom_call_target="tpu_custom_call" | custom-call | tf_op jit(solution)/shard_map/attend/pallas_call | solution.py:247
  172.8 4.1 %collective-permute-start.2 = (f32[24,128]{1,0:T(8,128)S(1)}, f32[24,128]{1,0:T(8,128)S(1)}, u32[]{:S(2)}, u32[]{:S(2)}) collective-permute-start(f32[24,128]{1,0:T(8,128)S(1)} %get-tuple-element.12.refs_2_), channel_id=1, source_target_pairs={{0,3},{1,0},{2,1},{3,2},{4,7},{5,4},{6,5},{7,6},{8,11},{9,8},{10,9... | collective-permute-start | bytes 36872 | tf_op jit(solution)/shard_map/ppermute | solution.py:307
  176.9 0.0 collective-permute-start.1
  176.9 1.3 collective-permute-start
  178.2 0.1 collective-permute-done.2.refs_5_
  178.3 3.8 %collective-permute-done.1.refs_4_ = f32[24,128]{1,0:T(8,128)S(1)} collective-permute-done((f32[24,128]{1,0:T(8,128)S(1)}, f32[24,128]{1,0:T(8,128)S(1)}, u32[]{:S(2)}, u32[]{:S(2)}) %collective-permute-start.1) | collective-permute-done | bytes 12320 | tf_op jit(solution)/shard_map/ppermute | solution.py:307
  182.1 0.0 collective-permute-done.refs_3_
  182.1 0.0 copy-done
  182.1 3.0 %finish_rows.1 = bf16[3072,1024]{1,0:T(8,128)(2,1)} custom-call(f32[3072,1024]{1,0:T(8,128)S(1)} %get-tuple-element.11.refs_0_, f32[1,1024]{1,0:T(1,128)S(1)} %bitcast.7, f32[24,128]{1,0:T(8,128)S(1)} %get-tuple-element.12.refs_2_, f32[24,128]{1,0:T(8,128)S(1)} %collective-permute-done.refs_3_, f32[24,128]{1,0:T(8,128)S(1)} %collective-permute-done.1.refs_4_, ...), custom_call_target="tpu_custom_call" | custom-call | tf_op jit(solution)/shard_map/finish_rows/pallas_call | solution.py:284
  (2 shorter events, 0.0 us)
Async XLA Ops:
  7.3 161.7 %slice-start = ((s8[6291456]{0:T(1024)(128)(4,1)}), s8[4194304]{0:T(1024)(128)(4,1)S(1)}, s32[]{:S(2)}) async-start(s8[6291456]{0:T(1024)(128)(4,1)} %bitcast.3), calls=%async_computation.2 | async-start | bytes 8388608
  7.3 161.6 %slice-start.2 = ((s8[6291456]{0:T(1024)(128)(4,1)}), s8[4194304]{0:T(1024)(128)(4,1)S(1)}, s32[]{:S(2)}) async-start(s8[6291456]{0:T(1024)(128)(4,1)} %bitcast.5), calls=%async_computation.4 | async-start | bytes 8388608
  88.5 80.5 %slice-start.1 = ((s8[6291456]{0:T(1024)(128)(4,1)}), s8[2097152]{0:T(1024)(128)(4,1)S(1)}, s32[]{:S(2)}) async-start(s8[6291456]{0:T(1024)(128)(4,1)} %bitcast.3), calls=%async_computation.3 | async-start | bytes 4194304
  88.5 80.5 %slice-start.3 = ((s8[6291456]{0:T(1024)(128)(4,1)}), s8[2097152]{0:T(1024)(128)(4,1)S(1)}, s32[]{:S(2)}) async-start(s8[6291456]{0:T(1024)(128)(4,1)} %bitcast.5), calls=%async_computation.5 | async-start | bytes 4194304
  169.0 13.1 %copy-start = (f32[1024]{0:T(1024)S(1)}, f32[1024]{0:T(1024)}, u32[]{:S(2)}) copy-start(f32[1024]{0:T(1024)} %param.9) | copy-start | bytes 12292
  172.8 5.5 %collective-permute-start.2 = (f32[24,128]{1,0:T(8,128)S(1)}, f32[24,128]{1,0:T(8,128)S(1)}, u32[]{:S(2)}, u32[]{:S(2)}) collective-permute-start(f32[24,128]{1,0:T(8,128)S(1)} %get-tuple-element.12.refs_2_), channel_id=1, source_target_pairs={{0,3},{1,0},{2,1},{3,2},{4,7},{5,4},{6,5},{7,6},{8,11},{9,8},{10,9... | collective-permute-start | bytes 36872 | tf_op jit(solution)/shard_map/ppermute | solution.py:307
  176.9 5.2 %collective-permute-start.1 = (f32[24,128]{1,0:T(8,128)S(1)}, f32[24,128]{1,0:T(8,128)S(1)}, u32[]{:S(2)}, u32[]{:S(2)}) collective-permute-start(f32[24,128]{1,0:T(8,128)S(1)} %get-tuple-element.12.refs_2_), channel_id=1, source_target_pairs={{0,2},{1,3},{2,0},{3,1},{4,6},{5,7},{6,4},{7,5},{8,10},{9,11},{10,... | collective-permute-start | bytes 36872 | tf_op jit(solution)/shard_map/ppermute | solution.py:307
  176.9 5.2 %collective-permute-start = (f32[24,128]{1,0:T(8,128)S(1)}, f32[24,128]{1,0:T(8,128)S(1)}, u32[]{:S(2)}, u32[]{:S(2)}) collective-permute-start(f32[24,128]{1,0:T(8,128)S(1)} %get-tuple-element.12.refs_2_), channel_id=1, source_target_pairs={{0,1},{1,2},{2,3},{3,0},{4,5},{5,6},{6,7},{7,4},{8,9},{9,10},{10,1... | collective-permute-start | bytes 36872 | tf_op jit(solution)/shard_map/ppermute | solution.py:307

commit v5 on v4

--- a/solution.py
+++ b/solution.py
@@ -16,11 +16,12 @@
 SLICE = FEATURES // SEQ
 PARTS = HD // SLICE
 SENT = BLOCKS_DEV * SLICE
-PLAN = 8
+PLAN = 16
 STEP = 3
 STEPS = BLOCKS_DEV // STEP
 ATTEND_STEP = 24
 GROUP = 24
+LOADED = 8
 OUT_AT = SEQ
 SEGMENT_AT = 2 * SEQ
 MIB = 1 << 20
@@ -176,17 +177,21 @@
             group = range(first, first + GROUP)
 
             def run(total, last, check):
-                loaded = [got_rows[rows_at(table[o, w], SLICE), :] for w in group]
-                before = []
-                for w, state in zip(group, loaded):
-                    if check:
-                        segment = table[o, SEGMENT_AT + w]
-                        total = jnp.where(segment == last, total, 0.0)
-                        last = segment
-                    before.append(total.astype(BF16))
-                    total = total + state.astype(F32)
-                for w, value in zip(group, before):
-                    out_rows[rows_at(table[o, OUT_AT + w], SLICE), :] = value
+                for start in range(group[0], group[-1] + 1, LOADED):
+                    part = range(start, start + LOADED)
+                    loaded = [
+                        got_rows[pl.ds(pl.multiple_of(table[o, w], PLAN), SLICE), :] for w in part
+                    ]
+                    before = []
+                    for w, state in zip(part, loaded):
+                        if check:
+                            segment = table[o, SEGMENT_AT + w]
+                            total = jnp.where(segment == last, total, 0.0)
+                            last = segment
+                        before.append(total.astype(BF16))
+                        total = total + state.astype(F32)
+                    for w, value in zip(part, before):
+                        out_rows[rows_at(table[o, OUT_AT + w], SLICE), :] = value
                 return total, last
 
             total, last = carry

time: 186 us -> 187 us (level)
  no operation moved by 1% of the time
where the time goes in v5:
time: 187 us; the launch traced here: 186 us
  blocking collectives  158 us (84%)
  Pallas kernels  18.1 us (10%)
  starting transfers between devices  5.37 us (3%)
  waiting for transfers between devices  3.94 us (2%)
    all_to_all x2, blocking collectives, to_all(): return lax.all_to_all(value, 'seq', split_axis=0, concat_axis=0, tiled=True)  158 us
    pallas_call x1, Pallas kernels, states(): pl.pallas_call(states_kernel, in_specs=[HBM] * 5, out_specs=[VMEM, VMEM],...  7.31 us
    ppermute x3, starting transfers between devices, on_device(): lax.ppermute(square, 'head', [(i, (i + s) % head_count) for i in range(he...  5.37 us
    pallas_call x1, Pallas kernels, prefix(): pl.pallas_call(prefix_kernel, in_specs=[VMEM], out_specs=VMEM, out_shape=...  4 us
    ppermute x3, waiting for transfers between devices, on_device(): lax.ppermute(square, 'head', [(i, (i + s) % head_count) for i in range(he...  3.94 us
    pallas_call x1, Pallas kernels, attend(): pl.pallas_call(attend_kernel, in_specs=[VMEM] * 4, out_specs=[VMEM, VMEM]...  3.77 us
  transfers between devices with their start and end apart: 3, of which 2 were waited for; matrix products, arithmetic and copies ran while one was open for 0% of the time, Pallas kernels for 0%

profile of v5, /device:TPU:8, one launch (start us, length us, event | category | flops | bytes accessed | tf_op | source)
XLA Modules:
  0.0 185.5 jit_solution(16099882393064597501)
XLA Ops:
  0.0 7.3 %block_states.1 = (bf16[32,784,128]{2,1,0:T(8,128)(2,1)S(1)}, bf16[3072,1024]{1,0:T(8,128)(2,1)S(1)}) custom-call(bf16[3072,1024]{1,0:T(8,128)(2,1)} %q_ref.3, bf16[3072,1024]{1,0:T(8,128)(2,1)} %k_ref.1, bf16[3072,1024]{1,0:T(8,128)(2,1)} %v_ref.3, s32[1,24]{1,0:T(1,128)} %bitcast.8, s32[1,24]{1,0:T(1,128)} %bitcast.9), custom_call_target="tpu_custom_call" | custom-call | tf_op jit(solution)/shard_map/block_states/pallas_call | solution.py:111
  7.3 0.0 slice-start
  7.3 0.0 slice-start.2
  7.3 81.6 %all_to_all.10.got_ref = bf16[32,784,128]{2,1,0:T(8,128)(2,1)S(1)} all-to-all(bf16[32,784,128]{2,1,0:T(8,128)(2,1)S(1)} %get-tuple-element.10), channel_id=1, replica_groups=mesh['seq'=32,'head'=4] {'seq'}, dimensions={0} | all-to-all | bytes 12845056 | tf_op jit(solution)/shard_map/all_to_all | solution.py:304
  89.0 0.0 slice-start.1
  89.0 0.0 slice-start.3
  89.0 4.0 %prefix.1 = bf16[32,768,128]{2,1,0:T(8,128)(2,1)S(1)} custom-call(bf16[32,784,128]{2,1,0:T(8,128)(2,1)S(1)} %all_to_all.10.got_ref), custom_call_target="tpu_custom_call" | custom-call | tf_op jit(solution)/shard_map/prefix/pallas_call | solution.py:211
  93.0 76.4 %all_to_all.11.carried_ref = bf16[32,768,128]{2,1,0:T(8,128)(2,1)S(1)} all-to-all(bf16[32,768,128]{2,1,0:T(8,128)(2,1)S(1)} %prefix.1), channel_id=1, replica_groups=mesh['seq'=32,'head'=4] {'seq'}, dimensions={0} | all-to-all | bytes 12582912 | tf_op jit(solution)/shard_map/all_to_all | solution.py:304
  169.4 0.0 slice-done
  169.4 0.0 slice-done.2
  169.4 0.0 slice-done.1
  169.4 0.0 slice-done.3
  169.4 0.0 copy-start
  169.4 3.8 %attend.1 = (f32[3072,1024]{1,0:T(8,128)S(1)}, f32[24,128]{1,0:T(8,128)S(1)}) custom-call(bf16[3072,1024]{1,0:T(8,128)(2,1)S(1)} %bitcast.4, bf16[3072,1024]{1,0:T(8,128)(2,1)S(1)} %get-tuple-element.9.scores_ref, bf16[3072,1024]{1,0:T(8,128)(2,1)S(1)} %bitcast.6, bf16[32,768,128]{2,1,0:T(8,128)(2,1)S(1)} %all_to_all.11.carried_ref), custom_call_target="tpu_custom_call" | custom-call | tf_op jit(solution)/shard_map/attend/pallas_call | solution.py:252
  173.2 4.1 %collective-permute-start.2 = (f32[24,128]{1,0:T(8,128)S(1)}, f32[24,128]{1,0:T(8,128)S(1)}, u32[]{:S(2)}, u32[]{:S(2)}) collective-permute-start(f32[24,128]{1,0:T(8,128)S(1)} %get-tuple-element.12.refs_2_), channel_id=1, source_target_pairs={{0,3},{1,0},{2,1},{3,2},{4,7},{5,4},{6,5},{7,6},{8,11},{9,8},{10,9... | collective-permute-start | bytes 36872 | tf_op jit(solution)/shard_map/ppermute | solution.py:312
  177.3 0.0 collective-permute-start.1
  177.3 1.3 collective-permute-start
  178.6 0.1 collective-permute-done.2.refs_5_
  178.7 3.8 %collective-permute-done.1.refs_4_ = f32[24,128]{1,0:T(8,128)S(1)} collective-permute-done((f32[24,128]{1,0:T(8,128)S(1)}, f32[24,128]{1,0:T(8,128)S(1)}, u32[]{:S(2)}, u32[]{:S(2)}) %collective-permute-start.1) | collective-permute-done | bytes 12320 | tf_op jit(solution)/shard_map/ppermute | solution.py:312
  182.5 0.0 collective-permute-done.refs_3_
  182.5 0.0 copy-done
  182.5 3.0 %finish_rows.1 = bf16[3072,1024]{1,0:T(8,128)(2,1)} custom-call(f32[3072,1024]{1,0:T(8,128)S(1)} %get-tuple-element.11.refs_0_, f32[1,1024]{1,0:T(1,128)S(1)} %bitcast.7, f32[24,128]{1,0:T(8,128)S(1)} %get-tuple-element.12.refs_2_, f32[24,128]{1,0:T(8,128)S(1)} %collective-permute-done.refs_3_, f32[24,128]{1,0:T(8,128)S(1)} %collective-permute-done.1.refs_4_, ...), custom_call_target="tpu_custom_call" | custom-call | tf_op jit(solution)/shard_map/finish_rows/pallas_call | solution.py:289
  (2 shorter events, 0.0 us)
Async XLA Ops:
  7.3 162.1 %slice-start = ((s8[6291456]{0:T(1024)(128)(4,1)}), s8[4194304]{0:T(1024)(128)(4,1)S(1)}, s32[]{:S(2)}) async-start(s8[6291456]{0:T(1024)(128)(4,1)} %bitcast.3), calls=%async_computation.2 | async-start | bytes 8388608
  7.3 162.0 %slice-start.2 = ((s8[6291456]{0:T(1024)(128)(4,1)}), s8[4194304]{0:T(1024)(128)(4,1)S(1)}, s32[]{:S(2)}) async-start(s8[6291456]{0:T(1024)(128)(4,1)} %bitcast.5), calls=%async_computation.4 | async-start | bytes 8388608
  89.0 80.4 %slice-start.1 = ((s8[6291456]{0:T(1024)(128)(4,1)}), s8[2097152]{0:T(1024)(128)(4,1)S(1)}, s32[]{:S(2)}) async-start(s8[6291456]{0:T(1024)(128)(4,1)} %bitcast.3), calls=%async_computation.3 | async-start | bytes 4194304
  89.0 80.4 %slice-start.3 = ((s8[6291456]{0:T(1024)(128)(4,1)}), s8[2097152]{0:T(1024)(128)(4,1)S(1)}, s32[]{:S(2)}) async-start(s8[6291456]{0:T(1024)(128)(4,1)} %bitcast.5), calls=%async_computation.5 | async-start | bytes 4194304
  169.4 13.1 %copy-start = (f32[1024]{0:T(1024)S(1)}, f32[1024]{0:T(1024)}, u32[]{:S(2)}) copy-start(f32[1024]{0:T(1024)} %param.9) | copy-start | bytes 12292
  173.2 5.5 %collective-permute-start.2 = (f32[24,128]{1,0:T(8,128)S(1)}, f32[24,128]{1,0:T(8,128)S(1)}, u32[]{:S(2)}, u32[]{:S(2)}) collective-permute-start(f32[24,128]{1,0:T(8,128)S(1)} %get-tuple-element.12.refs_2_), channel_id=1, source_target_pairs={{0,3},{1,0},{2,1},{3,2},{4,7},{5,4},{6,5},{7,6},{8,11},{9,8},{10,9... | collective-permute-start | bytes 36872 | tf_op jit(solution)/shard_map/ppermute | solution.py:312
  177.3 5.2 %collective-permute-start.1 = (f32[24,128]{1,0:T(8,128)S(1)}, f32[24,128]{1,0:T(8,128)S(1)}, u32[]{:S(2)}, u32[]{:S(2)}) collective-permute-start(f32[24,128]{1,0:T(8,128)S(1)} %get-tuple-element.12.refs_2_), channel_id=1, source_target_pairs={{0,2},{1,3},{2,0},{3,1},{4,6},{5,7},{6,4},{7,5},{8,10},{9,11},{10,... | collective-permute-start | bytes 36872 | tf_op jit(solution)/shard_map/ppermute | solution.py:312
  177.3 5.2 %collective-permute-start = (f32[24,128]{1,0:T(8,128)S(1)}, f32[24,128]{1,0:T(8,128)S(1)}, u32[]{:S(2)}, u32[]{:S(2)}) collective-permute-start(f32[24,128]{1,0:T(8,128)S(1)} %get-tuple-element.12.refs_2_), channel_id=1, source_target_pairs={{0,1},{1,2},{2,3},{3,0},{4,5},{5,6},{6,7},{7,4},{8,9},{9,10},{10,1... | collective-permute-start | bytes 36872 | tf_op jit(solution)/shard_map/ppermute | solution.py:312

commit v6 on v5

--- a/solution.py
+++ b/solution.py
@@ -92,7 +92,7 @@
                 scores_ref[rows, head_cols(h)] = jnp.where(causal, scores, 0.0).astype(BF16)
         return carry
 
-    lax.fori_loop(0, STEPS, step, 0)
+    lax.fori_loop(0, STEPS - 1, step, 0)
     place_copy.wait()
     segment_copy.wait()
     place = given[0]
@@ -104,6 +104,7 @@
     own_ref[:, SENT : SENT + PLAN] = jnp.broadcast_to(
         plan[...].astype(F32).astype(BF16)[None], (SEQ, PLAN, HD)
     )
+    lax.fori_loop(STEPS - 1, STEPS, step, 0)
 
 
 def states(queries, keys, values, placement, segments):

time: 187 us -> 187 us (level)
  no operation moved by 1% of the time
where the time goes in v6:
time: 187 us; the launch traced here: 186 us
  blocking collectives  158 us (84%)
  Pallas kernels  18.1 us (10%)
  starting transfers between devices  5.37 us (3%)
  waiting for transfers between devices  3.94 us (2%)
    all_to_all x2, blocking collectives, to_all(): return lax.all_to_all(value, 'seq', split_axis=0, concat_axis=0, tiled=True)  158 us
    pallas_call x1, Pallas kernels, states(): pl.pallas_call(states_kernel, in_specs=[HBM] * 5, out_specs=[VMEM, VMEM],...  7.25 us
    ppermute x3, starting transfers between devices, on_device(): lax.ppermute(square, 'head', [(i, (i + s) % head_count) for i in range(he...  5.37 us
    pallas_call x1, Pallas kernels, prefix(): pl.pallas_call(prefix_kernel, in_specs=[VMEM], out_specs=VMEM, out_shape=...  4.04 us
    ppermute x3, waiting for transfers between devices, on_device(): lax.ppermute(square, 'head', [(i, (i + s) % head_count) for i in range(he...  3.94 us
    pallas_call x1, Pallas kernels, attend(): pl.pallas_call(attend_kernel, in_specs=[VMEM] * 4, out_specs=[VMEM, VMEM]...  3.77 us
  transfers between devices with their start and end apart: 3, of which 2 were waited for; matrix products, arithmetic and copies ran while one was open for 0% of the time, Pallas kernels for 0%

profile of v6, /device:TPU:8, one launch (start us, length us, event | category | flops | bytes accessed | tf_op | source)
XLA Modules:
  0.0 185.5 jit_solution(1375886318545322196)
XLA Ops:
  0.0 7.2 %block_states.1 = (bf16[32,784,128]{2,1,0:T(8,128)(2,1)S(1)}, bf16[3072,1024]{1,0:T(8,128)(2,1)S(1)}) custom-call(bf16[3072,1024]{1,0:T(8,128)(2,1)} %q_ref.3, bf16[3072,1024]{1,0:T(8,128)(2,1)} %k_ref.1, bf16[3072,1024]{1,0:T(8,128)(2,1)} %v_ref.3, s32[1,24]{1,0:T(1,128)} %bitcast.8, s32[1,24]{1,0:T(1,128)} %bitcast.9), custom_call_target="tpu_custom_call" | custom-call | tf_op jit(solution)/shard_map/block_states/pallas_call | solution.py:112
  7.3 0.0 slice-start
  7.3 0.0 slice-start.2
  7.3 81.6 %all_to_all.10.got_ref = bf16[32,784,128]{2,1,0:T(8,128)(2,1)S(1)} all-to-all(bf16[32,784,128]{2,1,0:T(8,128)(2,1)S(1)} %get-tuple-element.10), channel_id=1, replica_groups=mesh['seq'=32,'head'=4] {'seq'}, dimensions={0} | all-to-all | bytes 12845056 | tf_op jit(solution)/shard_map/all_to_all | solution.py:305
  88.9 0.0 slice-start.1
  88.9 0.0 slice-start.3
  88.9 4.0 %prefix.1 = bf16[32,768,128]{2,1,0:T(8,128)(2,1)S(1)} custom-call(bf16[32,784,128]{2,1,0:T(8,128)(2,1)S(1)} %all_to_all.10.got_ref), custom_call_target="tpu_custom_call" | custom-call | tf_op jit(solution)/shard_map/prefix/pallas_call | solution.py:212
  92.9 76.4 %all_to_all.11.carried_ref = bf16[32,768,128]{2,1,0:T(8,128)(2,1)S(1)} all-to-all(bf16[32,768,128]{2,1,0:T(8,128)(2,1)S(1)} %prefix.1), channel_id=1, replica_groups=mesh['seq'=32,'head'=4] {'seq'}, dimensions={0} | all-to-all | bytes 12582912 | tf_op jit(solution)/shard_map/all_to_all | solution.py:305
  169.3 0.0 slice-done
  169.3 0.0 slice-done.2
  169.3 0.0 slice-done.1
  169.4 0.0 slice-done.3
  169.4 0.0 copy-start
  169.4 3.8 %attend.1 = (f32[3072,1024]{1,0:T(8,128)S(1)}, f32[24,128]{1,0:T(8,128)S(1)}) custom-call(bf16[3072,1024]{1,0:T(8,128)(2,1)S(1)} %bitcast.4, bf16[3072,1024]{1,0:T(8,128)(2,1)S(1)} %get-tuple-element.9.scores_ref, bf16[3072,1024]{1,0:T(8,128)(2,1)S(1)} %bitcast.6, bf16[32,768,128]{2,1,0:T(8,128)(2,1)S(1)} %all_to_all.11.carried_ref), custom_call_target="tpu_custom_call" | custom-call | tf_op jit(solution)/shard_map/attend/pallas_call | solution.py:253
  173.2 4.1 %collective-permute-start.2 = (f32[24,128]{1,0:T(8,128)S(1)}, f32[24,128]{1,0:T(8,128)S(1)}, u32[]{:S(2)}, u32[]{:S(2)}) collective-permute-start(f32[24,128]{1,0:T(8,128)S(1)} %get-tuple-element.12.refs_2_), channel_id=1, source_target_pairs={{0,3},{1,0},{2,1},{3,2},{4,7},{5,4},{6,5},{7,6},{8,11},{9,8},{10,9... | collective-permute-start | bytes 36872 | tf_op jit(solution)/shard_map/ppermute | solution.py:313
  177.3 0.0 collective-permute-start.1
  177.3 1.3 collective-permute-start
  178.5 0.1 collective-permute-done.2.refs_5_
  178.7 3.8 %collective-permute-done.1.refs_4_ = f32[24,128]{1,0:T(8,128)S(1)} collective-permute-done((f32[24,128]{1,0:T(8,128)S(1)}, f32[24,128]{1,0:T(8,128)S(1)}, u32[]{:S(2)}, u32[]{:S(2)}) %collective-permute-start.1) | collective-permute-done | bytes 12320 | tf_op jit(solution)/shard_map/ppermute | solution.py:313
  182.5 0.0 collective-permute-done.refs_3_
  182.5 0.0 copy-done
  182.5 3.0 %finish_rows.1 = bf16[3072,1024]{1,0:T(8,128)(2,1)} custom-call(f32[3072,1024]{1,0:T(8,128)S(1)} %get-tuple-element.11.refs_0_, f32[1,1024]{1,0:T(1,128)S(1)} %bitcast.7, f32[24,128]{1,0:T(8,128)S(1)} %get-tuple-element.12.refs_2_, f32[24,128]{1,0:T(8,128)S(1)} %collective-permute-done.refs_3_, f32[24,128]{1,0:T(8,128)S(1)} %collective-permute-done.1.refs_4_, ...), custom_call_target="tpu_custom_call" | custom-call | tf_op jit(solution)/shard_map/finish_rows/pallas_call | solution.py:290
  (2 shorter events, 0.0 us)
Async XLA Ops:
  7.3 162.1 %slice-start = ((s8[6291456]{0:T(1024)(128)(4,1)}), s8[4194304]{0:T(1024)(128)(4,1)S(1)}, s32[]{:S(2)}) async-start(s8[6291456]{0:T(1024)(128)(4,1)} %bitcast.3), calls=%async_computation.2 | async-start | bytes 8388608
  7.3 162.1 %slice-start.2 = ((s8[6291456]{0:T(1024)(128)(4,1)}), s8[4194304]{0:T(1024)(128)(4,1)S(1)}, s32[]{:S(2)}) async-start(s8[6291456]{0:T(1024)(128)(4,1)} %bitcast.5), calls=%async_computation.4 | async-start | bytes 8388608
  88.9 80.5 %slice-start.1 = ((s8[6291456]{0:T(1024)(128)(4,1)}), s8[2097152]{0:T(1024)(128)(4,1)S(1)}, s32[]{:S(2)}) async-start(s8[6291456]{0:T(1024)(128)(4,1)} %bitcast.3), calls=%async_computation.3 | async-start | bytes 4194304
  88.9 80.5 %slice-start.3 = ((s8[6291456]{0:T(1024)(128)(4,1)}), s8[2097152]{0:T(1024)(128)(4,1)S(1)}, s32[]{:S(2)}) async-start(s8[6291456]{0:T(1024)(128)(4,1)} %bitcast.5), calls=%async_computation.5 | async-start | bytes 4194304
  169.4 13.1 %copy-start = (f32[1024]{0:T(1024)S(1)}, f32[1024]{0:T(1024)}, u32[]{:S(2)}) copy-start(f32[1024]{0:T(1024)} %param.9) | copy-start | bytes 12292
  173.2 5.5 %collective-permute-start.2 = (f32[24,128]{1,0:T(8,128)S(1)}, f32[24,128]{1,0:T(8,128)S(1)}, u32[]{:S(2)}, u32[]{:S(2)}) collective-permute-start(f32[24,128]{1,0:T(8,128)S(1)} %get-tuple-element.12.refs_2_), channel_id=1, source_target_pairs={{0,3},{1,0},{2,1},{3,2},{4,7},{5,4},{6,5},{7,6},{8,11},{9,8},{10,9... | collective-permute-start | bytes 36872 | tf_op jit(solution)/shard_map/ppermute | solution.py:313
  177.3 5.2 %collective-permute-start.1 = (f32[24,128]{1,0:T(8,128)S(1)}, f32[24,128]{1,0:T(8,128)S(1)}, u32[]{:S(2)}, u32[]{:S(2)}) collective-permute-start(f32[24,128]{1,0:T(8,128)S(1)} %get-tuple-element.12.refs_2_), channel_id=1, source_target_pairs={{0,2},{1,3},{2,0},{3,1},{4,6},{5,7},{6,4},{7,5},{8,10},{9,11},{10,... | collective-permute-start | bytes 36872 | tf_op jit(solution)/shard_map/ppermute | solution.py:313
  177.3 5.2 %collective-permute-start = (f32[24,128]{1,0:T(8,128)S(1)}, f32[24,128]{1,0:T(8,128)S(1)}, u32[]{:S(2)}, u32[]{:S(2)}) collective-permute-start(f32[24,128]{1,0:T(8,128)S(1)} %get-tuple-element.12.refs_2_), channel_id=1, source_target_pairs={{0,1},{1,2},{2,3},{3,0},{4,5},{5,6},{6,7},{7,4},{8,9},{9,10},{10,1... | collective-permute-start | bytes 36872 | tf_op jit(solution)/shard_map/ppermute | solution.py:313
